TPU v7x, 256 devices: a whole 4x4x8 slice. The times are simulated.
256 devices in a mesh: pipe: 32 (over x_lo, z, core), ctx: 8 (over y, x_hi).
Axes of the slice: x: 4 (x_hi: 2, x_lo: 2; x = x_hi * 2 + x_lo), y: 4, z: 8, core: 2. Of those that a mesh axis runs over, the one named last changes fastest.
Arguments:
- inflow: bfloat16 [32, 2, 512, 3072], P('pipe', None, 'ctx'), may hold values from -6 to 6
- patches: bfloat16 [2, 512, 64], P(None, 'ctx'), may hold values from -6 to 6
- patch_weight: bfloat16 [64, 3072], replicated, may hold values from -0.75 to 0.75
- timesteps: int32 [2], replicated, may hold values from 0 to 999
- time_weight: bfloat16 [256, 3072], replicated, may hold values from -0.375 to 0.375
- mod_weight: bfloat16 [3072, 9216], P(('pipe', 'ctx')), may hold values from -0.109375 to 0.109375
- layer_table: bfloat16 [32, 9216], replicated, may hold values from -3 to 3
- section_layer: int32 [32], replicated, may hold values from 0 to 31, each once
- token_cell: int32 [512], replicated, may hold values from 0 to 511, each once
- q_weight: bfloat16 [32, 3072, 3072], P('pipe', None, 'ctx')
- k_weight: bfloat16 [32, 3072, 3072], P('pipe', None, 'ctx')
- v_weight: bfloat16 [32, 3072, 3072], P('pipe', None, 'ctx'), may hold values from -0.109375 to 0.109375
- out_weight: bfloat16 [32, 3072, 3072], P('pipe', 'ctx'), may hold values from -0.625 to 0.625
- q_gain: float32 [32, 3072], P('pipe', 'ctx'), may hold values from 0.6 to 5
- k_gain: float32 [32, 3072], P('pipe', 'ctx'), may hold values from 0.6 to 5
Outputs:
- handed_off: bfloat16 [32, 2, 512, 3072], P('pipe', None, 'ctx')
Inputs may be any that keep to these rules, and one draw needn't show every extreme that they name: `section_layer`: each section runs a different layer. `token_cell`: each cell of the 512-token grid holds one token.
All inputs are finite; a program needn't handle non-finite values.
Results may differ from a plain program's by a relative error of at most 0.02.
Values may be sent and summed in bfloat16 or wider, within the bound.
A program may use at most 128 MiB of HBM per device.

v0:
```python
import math

import jax
import jax.numpy as jnp
from jax import lax
from jax.sharding import PartitionSpec as P

HEAD = 128
GRID_H = 8
GRID_W = 16


def passed_along(value, axis, steps):
    count = lax.axis_size(axis)
    first, last = (max(0, -steps), min(count, count - steps))
    return lax.ppermute(value, axis, [(source, source + steps) for source in range(first, last)])


def time_features(timesteps, freq_count):
    half_size = freq_count // 2
    rates = 10000.0 ** (-jnp.arange(half_size, dtype=jnp.float32) / half_size)
    angles = timesteps.astype(jnp.float32)[:, None] * rates[None, :]
    return jnp.concatenate([jnp.cos(angles), jnp.sin(angles)], 1).astype(jnp.bfloat16)


def rope_tables(token_cell):
    half_size = HEAD // 2
    time_pairs = half_size - 2 * (HEAD // 6)
    space_pairs = HEAD // 6
    frame_pos = token_cell // (GRID_H * GRID_W)
    row_pos = token_cell // GRID_W % GRID_H
    col_pos = token_cell % GRID_W
    pair_ids = jnp.arange(half_size, dtype=jnp.int32)
    positions = jnp.where(
        pair_ids[None, :] < time_pairs,
        frame_pos[:, None],
        jnp.where(pair_ids[None, :] < time_pairs + space_pairs, row_pos[:, None], col_pos[:, None]),
    )
    pair_float = pair_ids.astype(jnp.float32)
    exponent = jnp.where(
        pair_ids < time_pairs,
        pair_float / time_pairs,
        jnp.where(
            pair_ids < time_pairs + space_pairs,
            (pair_float - time_pairs) / space_pairs,
            (pair_float - time_pairs - space_pairs) / space_pairs,
        ),
    )
    angles = positions.astype(jnp.float32) * (10000.0 ** (-exponent))[None, :]
    return (jnp.cos(angles), jnp.sin(angles))


def rotate(heads_in, cos_table, sin_table):
    half_size = heads_in.shape[-1] // 2
    first_half = heads_in[..., :half_size]
    second_half = heads_in[..., half_size:]
    cos_b = cos_table[:, None, :]
    sin_b = sin_table[:, None, :]
    return jnp.concatenate(
        [first_half * cos_b - second_half * sin_b, first_half * sin_b + second_half * cos_b], -1
    )


def modulated_norm(row_block, shift_mod, scale_mod):
    values_f = row_block.astype(jnp.float32)
    center = values_f - jnp.mean(values_f, -1, keepdims=True)
    spread = jnp.mean(center * center, -1, keepdims=True)
    return (center * lax.rsqrt(spread + 1e-06) * (1.0 + scale_mod) + shift_mod).astype(jnp.bfloat16)


def project_three(normed, w_query, w_key, w_value):
    return jnp.concatenate(
        [
            jnp.dot(normed, w_query, preferred_element_type=jnp.float32),
            jnp.dot(normed, w_key, preferred_element_type=jnp.float32),
            jnp.dot(normed, w_value, preferred_element_type=jnp.float32),
        ],
        1,
    )


def attend(queries, keys_all, val_heads):
    total_rows = queries.shape[0]
    block_rows = math.gcd(total_rows, 512)
    local_heads = queries.shape[1]
    query_blocks = queries.reshape(total_rows // block_rows, block_rows, local_heads, HEAD)

    def one_block(query_rows):
        scores = jnp.einsum(
            "thd,shd->hts", query_rows, keys_all, preferred_element_type=jnp.float32
        ) * HEAD ** (-0.5)
        scores = scores - jnp.max(scores, -1, keepdims=True)
        weights = jnp.exp(scores)
        probs = (weights / jnp.sum(weights, -1, keepdims=True)).astype(jnp.bfloat16)
        return jnp.einsum(
            "hts,shd->thd", probs, val_heads, preferred_element_type=jnp.float32
        ).astype(jnp.bfloat16)

    attended = lax.map(one_block, query_blocks)
    return attended.reshape(total_rows, local_heads * HEAD)


def shards(
    inflow,
    patches,
    patch_weight,
    timesteps,
    time_weight,
    mod_weight,
    layer_table,
    section_layer,
    token_cell,
    q_weight,
    k_weight,
    v_weight,
    out_weight,
    q_gain,
    k_gain,
):
    micro_count = inflow.shape[1]
    width = inflow.shape[3]
    local_cols = q_weight.shape[2]
    local_heads = local_cols // HEAD
    total_cols = local_cols * lax.axis_size("ctx")
    section = lax.axis_index("pipe")
    time_hidden = jax.nn.silu(
        jnp.dot(
            time_features(timesteps, time_weight.shape[0]),
            time_weight,
            preferred_element_type=jnp.float32,
        )
    ).astype(jnp.bfloat16)
    share_rows = mod_weight.shape[0]
    flat_rank = lax.axis_index(("pipe", "ctx"))
    time_piece = lax.dynamic_slice_in_dim(time_hidden, flat_rank * share_rows, share_rows, 1)
    mod_base = lax.psum(
        jnp.dot(time_piece, mod_weight, preferred_element_type=jnp.float32), ("pipe", "ctx")
    )
    section_ids = jnp.arange(section_layer.shape[0], dtype=jnp.int32)
    layer_id = jnp.sum(jnp.where(section_ids == section, section_layer, 0))
    layer_row = jnp.sum(
        jnp.where((section_ids == layer_id)[:, None], layer_table.astype(jnp.float32), 0.0), 0
    )
    modulation = mod_base + layer_row[None, :]
    shift_all = modulation[:, :width]
    scale_all = modulation[:, width : 2 * width]
    gate_all = modulation[:, 2 * width :]
    embedded = jnp.einsum(
        "btp,pd->btd", patches, patch_weight, preferred_element_type=jnp.float32
    ).astype(jnp.bfloat16)
    start_block = jnp.where(section == 0, embedded, inflow[0])
    cos_table, sin_table = rope_tables(token_cell)
    w_query = q_weight[0]
    w_key = k_weight[0]
    w_value = v_weight[0]
    gain_query = q_gain[0]
    gain_key = k_gain[0]
    results = []
    for slot_index in range(micro_count):
        stream = start_block[slot_index]
        shift_mod = shift_all[slot_index]
        scale_mod = scale_all[slot_index]
        gate_mod = gate_all[slot_index]
        projected = project_three(
            modulated_norm(lax.all_gather(stream, "ctx", axis=0, tiled=True), shift_mod, scale_mod),
            w_query,
            w_key,
            w_value,
        )
        q_raw = projected[:, :local_cols]
        k_raw = projected[:, local_cols : 2 * local_cols]
        val_all = projected[:, 2 * local_cols :].astype(jnp.bfloat16)
        q_squares, k_squares = lax.psum(
            (jnp.sum(q_raw * q_raw, -1), jnp.sum(k_raw * k_raw, -1)), "ctx"
        )
        q_raw = q_raw * lax.rsqrt(q_squares / total_cols + 1e-06)[:, None] * gain_query
        k_raw = k_raw * lax.rsqrt(k_squares / total_cols + 1e-06)[:, None] * gain_key
        all_rows = q_raw.shape[0]
        queries = rotate(q_raw.reshape(all_rows, local_heads, HEAD), cos_table, sin_table).astype(
            jnp.bfloat16
        )
        keys_all = rotate(k_raw.reshape(all_rows, local_heads, HEAD), cos_table, sin_table).astype(
            jnp.bfloat16
        )
        attended = attend(queries, keys_all, val_all.reshape(all_rows, local_heads, HEAD))
        w_out = out_weight[0]
        branch = lax.psum_scatter(
            jnp.dot(attended, w_out, preferred_element_type=jnp.float32).astype(jnp.bfloat16),
            "ctx",
            scatter_dimension=0,
            tiled=True,
        ).astype(jnp.float32)
        section_out = (stream.astype(jnp.float32) + gate_mod[None, :] * branch).astype(jnp.bfloat16)
        results.append(section_out)
    stacked = jnp.stack(results)
    stacked = passed_along(stacked, "pipe", 1)
    return stacked[None]


def solution(mesh):
    placed = (
        P("pipe", None, "ctx", None),
        P(None, "ctx", None),
        P(),
        P(),
        P(),
        P(("pipe", "ctx"), None),
        P(),
        P(),
        P(),
        P("pipe", None, "ctx"),
        P("pipe", None, "ctx"),
        P("pipe", None, "ctx"),
        P("pipe", "ctx", None),
        P("pipe", "ctx"),
        P("pipe", "ctx"),
    )
    return jax.shard_map(
        shards, mesh=mesh, in_specs=placed, out_specs=P("pipe", None, "ctx", None), check_vma=False
    )
```

profile of v0, /device:TPU:5, one launch (start us, length us, event | category | flops | bytes accessed | tf_op | source)
XLA Modules:
  0.0 549.8 jit_solution(3839924708541463479)
XLA Ops:
  8.4 1.7 fusion.82
  10.1 1.9 fusion.89
  12.0 1.6 fusion.16
  13.7 1.0 fusion.108
  16.7 1.3 select_reduce_fusion
  18.1 2.1 fusion.69
  20.2 256.4 %all-reduce.3.cloned.1.call-done = f32[2,9216]{1,0:T(2,128)} async-done(((f32[2,9216]{1,0:T(2,128)}), f32[2,9216]{1,0:T(2,128)}) %all-reduce.3.cloned.1.call-update) | async-done | bytes 73744 | tf_op jit(solution)/shard_map/psum | solution.py:136
  276.5 0.9 broadcast_add_fusion
  278.1 2.5 convert_reduce_fusion
  281.0 1.0 fusion.12
  282.0 2.5 convert_reduce_fusion.1
  284.8 1.0 fusion.5
  285.8 1.8 fusion.8
  287.6 2.3 multiply_reduce_fusion.4
  289.9 2.3 multiply_reduce_fusion.5
  292.2 1.8 fusion.15
  294.1 2.3 multiply_reduce_fusion.2
  296.4 2.3 multiply_reduce_fusion.3
  298.7 2.2 fusion.43
  300.9 17.6 %all-reduce = (f32[512]{0:T(512)S(1)}, f32[512]{0:T(512)S(1)}, f32[512]{0:T(512)S(1)}, f32[512]{0:T(512)S(1)}) all-reduce(f32[512]{0:T(512)S(1)} %get-tuple-element.82, f32[512]{0:T(512)S(1)} %get-tuple-element.84, f32[512]{0:T(512)S(1)} %get-tuple-element.86, f32[512]{0:T(512)S(1)} %get-tuple-element.88), channel_id=1, replica_groups=mesh['pipe'=32,'ctx'=8] {'ctx'}, use_global_device_ids=true, to_apply=%region_15.16 | all-reduce | flops 2048 | bytes 16384 | tf_op jit(solution)/shard_map/psum | solution.py:173
  318.6 1.7 multiply_multiply_fusion.3
  321.2 1.0 fusion.105
  322.4 1.0 fusion.106
  323.3 1.0 fusion.104
  324.3 2.1 copy.30
  326.5 2.1 copy.34
  328.6 2.2 copy.28
  330.8 2.2 copy.32
  333.0 2.1 copy.31
  335.1 2.2 copy.35
  337.3 2.1 copy.29
  339.4 1.2 copy.33
  340.6 4.7 subtract_convert_fusion.2
  346.1 1.7 copy-done.5
  347.7 1.5 fusion.110
  349.2 5.0 fusion.42
  354.2 4.5 convolution_convert_fusion.1
  359.1 2.1 fusion.60
  361.1 1.7 copy-done.4
  362.8 1.4 fusion.111
  364.7 1.4 fusion.46
  366.1 4.8 fusion.41
  371.0 4.5 convolution_convert_fusion
  375.5 62.8 %reduce-scatter.3.cloned.1.call-done = bf16[64,3072]{1,0:T(8,128)(2,1)} async-done(((bf16[512,3072]{1,0:T(8,128)(2,1)}), bf16[64,3072]{1,0:T(8,128)(2,1)}) %reduce-scatter.3.cloned.1.call-update) | async-done | bytes 393232 | tf_op jit(solution)/shard_map/reduce_scatter | solution.py:187
  438.3 87.5 %reduce-scatter.5.cloned.1.call-done = bf16[64,3072]{1,0:T(8,128)(2,1)} async-done(((bf16[512,3072]{1,0:T(8,128)(2,1)}), bf16[64,3072]{1,0:T(8,128)(2,1)}) %reduce-scatter.5.cloned.1.call-update) | async-done | bytes 393232 | tf_op jit(solution)/shard_map/reduce_scatter | solution.py:187
  525.8 1.4 fusion.51
  527.3 5.2 collective-permute-start
  532.4 8.9 %collective-permute-done = bf16[2,64,3072]{2,1,0:T(8,128)(2,1)S(1)} collective-permute-done((bf16[2,64,3072]{2,1,0:T(8,128)(2,1)S(1)}, bf16[2,64,3072]{2,1,0:T(8,128)(2,1)S(1)}, u32[]{:S(2)}, u32[]{:S(2)}) %collective-permute-start) | collective-permute-done | bytes 786464 | tf_op jit(solution)/shard_map/ppermute | solution.py:16
  (70 shorter events, 7.9 us)
Async XLA Ops:
  7.4 346.9 %copy-start = (bf16[1,384,3072]{2,1,0:T(8,128)(2,1)S(1)}, bf16[1,384,3072]{2,1,0:T(8,128)(2,1)}, u32[]{:S(2)}) copy-start(bf16[1,384,3072]{2,1,0:T(8,128)(2,1)} %param.27) | copy-start | bytes 7077892
  7.4 269.2 %all-reduce.3.cloned.1.call-start = ((), (), s32[]{:S(2)}) async-start(), calls=%async_computation.2 | async-start | bytes 147456 | tf_op jit(solution)/shard_map/psum | solution.py:136
  8.3 7.0 %copy-start.12 = (f32[1,384]{1,0:T(1,128)S(1)}, f32[1,384]{1,0:T(1,128)}, u32[]{:S(2)}) copy-start(f32[1,384]{1,0:T(1,128)} %param.28) | copy-start | bytes 4612
  8.3 7.0 %copy-start.13 = (f32[1,384]{1,0:T(1,128)S(1)}, f32[1,384]{1,0:T(1,128)}, u32[]{:S(2)}) copy-start(f32[1,384]{1,0:T(1,128)} %param.29) | copy-start | bytes 4612
  8.3 7.0 %copy-start.18 = (s32[32]{0:T(128)S(1)}, s32[32]{0:T(128)}, u32[]{:S(2)}) copy-start(s32[32]{0:T(128)} %param.22) | copy-start | bytes 388
  8.3 9.7 %copy-start.11 = (s32[512]{0:T(512)S(1)}, s32[512]{0:T(512)}, u32[]{:S(2)}) copy-start(s32[512]{0:T(512)} %param.23) | copy-start | bytes 6148
  12.0 266.1 %all-gather.7.cloned.1.call-start = ((), (), s32[]{:S(2)}) async-start(), calls=%async_computation.6 | async-start | bytes 3538944 | tf_op jit(solution)/shard_map/all_gather | solution.py:165
  14.6 267.3 %all-gather.5.cloned.1.call-start = ((), (), s32[]{:S(2)}) async-start(), calls=%async_computation.5 | async-start | bytes 3538944 | tf_op jit(solution)/shard_map/all_gather | solution.py:165
  15.2 423.1 %reduce-scatter.3.cloned.1.call-start = ((), (), s32[]{:S(2)}) async-start(), calls=%async_computation.3 | async-start | bytes 3538944 | tf_op jit(solution)/shard_map/reduce_scatter | solution.py:187
  278.1 2.8 copy-start.1
  282.0 2.8 copy-start.3
  285.8 1.8 copy-start.14
  287.6 2.3 copy-start.15
  289.9 2.3 copy-start.2
  294.1 2.3 copy-start.6
  296.4 2.3 copy-start.16
  318.6 3.6 copy-start.8
  318.6 3.5 copy-start.9
  346.0 1.7 copy-start.5
  358.8 167.1 %reduce-scatter.5.cloned.1.call-start = ((), (), s32[]{:S(2)}) async-start(), calls=%async_computation.4 | async-start | bytes 3538944 | tf_op jit(solution)/shard_map/reduce_scatter | solution.py:187
  359.1 5.2 copy-start.17
  361.1 1.7 copy-start.4
  362.8 1.9 copy-start.7
  371.0 154.9 %copy-start.10 = (f32[1,3072]{1,0:T(1,128)S(1)}, f32[1,3072]{1,0:T(1,128)}, u32[]{:S(2)}) copy-start(f32[1,3072]{1,0:T(1,128)} %get-tuple-element.68) | copy-start | bytes 36868
  527.3 14.1 %collective-permute-start = (bf16[2,64,3072]{2,1,0:T(8,128)(2,1)S(1)}, bf16[2,64,3072]{2,1,0:T(8,128)(2,1)S(1)}, u32[]{:S(2)}, u32[]{:S(2)}) collective-permute-start(bf16[2,64,3072]{2,1,0:T(8,128)(2,1)S(1)} %pad_maximum_fusion), channel_id=1, source_target_pairs={{0,8},{8,16},{16,24},{24,32},{32,40},{40,48},{48,56},{56,64},{64,7... | collective-permute-start | bytes 2359304 | tf_op jit(solution)/shard_map/ppermute | solution.py:16
Sparse Core Ops, SparseCore 0:
  13.7 262.8 all-reduce.2
Sparse Core Ops, SparseCore 1:
  15.0 67.4 all-gather.6
  84.9 65.3 all-gather.4
  358.9 79.4 reduce-scatter.2
  442.5 83.3 reduce-scatter.4
where the time goes:
time: 555 us; the launch traced here: 550 us
  waiting for transfers between devices  416 us (75%)
  matrix products  39.7 us (7%)
  other arithmetic  28.9 us (5%)
  local copies, waits for them, and re-layouts  26.4 us (5%)
  blocking collectives  17.6 us (3%)
  between operations  15.4 us (3%)
  starting transfers between devices  5.55 us (1%)
    psum x1, waiting for transfers between devices, shards(): lax.psum(jnp.dot(time_piece, mod_weight, preferred_element_type=jnp.float...  256 us
    reduce_scatter x2, waiting for transfers between devices, shards(): lax.psum_scatter(jnp.dot(attended, w_out, preferred_element_type=jnp.floa...  150 us
    unnamed x47, local copies, waits for them, and re-layouts  21.7 us
    psum x1, blocking collectives, shards(): lax.psum((jnp.sum(q_raw * q_raw, -1), jnp.sum(k_raw * k_raw, -1)), 'ctx')  17.6 us
  transfers between devices with their start and end apart: 6, of which 4 were waited for; matrix products, arithmetic and copies ran while one was open for 5% of the time, Pallas kernels for 0%

commit v1 on v0

v1 whole, which is shorter than its diff:
```python
import functools

import jax
import jax.numpy as jnp
from jax import lax
from jax.experimental import pallas as pl
from jax.experimental.pallas import tpu as pltpu
from jax.sharding import PartitionSpec as P

HEAD = 128
GRID_H = 8
GRID_W = 16
MESH = pl.DeviceIdType.MESH
CTX = 8
CHUNK = 16

GATHER = 0
REDUCE = 8
STATS = 16
HAND = 23
PER_CLIP = 24


def time_features(timesteps, freq_count):
    half_size = freq_count // 2
    rates = 10000.0 ** (-jnp.arange(half_size, dtype=jnp.float32) / half_size)
    angles = timesteps.astype(jnp.float32)[:, None] * rates[None, :]
    return jnp.concatenate([jnp.cos(angles), jnp.sin(angles)], 1).astype(jnp.bfloat16)


def rope_tables(token_cell):
    half_size = HEAD // 2
    time_pairs = half_size - 2 * (HEAD // 6)
    space_pairs = HEAD // 6
    frame_pos = token_cell // (GRID_H * GRID_W)
    row_pos = token_cell // GRID_W % GRID_H
    col_pos = token_cell % GRID_W
    pair_ids = jnp.arange(half_size, dtype=jnp.int32)
    positions = jnp.where(
        pair_ids[None, :] < time_pairs,
        frame_pos[:, None],
        jnp.where(pair_ids[None, :] < time_pairs + space_pairs, row_pos[:, None], col_pos[:, None]),
    )
    pair_float = pair_ids.astype(jnp.float32)
    exponent = jnp.where(
        pair_ids < time_pairs,
        pair_float / time_pairs,
        jnp.where(
            pair_ids < time_pairs + space_pairs,
            (pair_float - time_pairs) / space_pairs,
            (pair_float - time_pairs - space_pairs) / space_pairs,
        ),
    )
    angles = positions.astype(jnp.float32) * (10000.0 ** (-exponent))[None, :]
    cos_half, sin_half = jnp.cos(angles), jnp.sin(angles)
    return jnp.concatenate([cos_half, cos_half], 1), jnp.concatenate([-sin_half, sin_half], 1)


def section_kernel(
    pipe_count,
    stream_in,
    mod_part,
    layer_row,
    cos_ref,
    sin_ref,
    q_weight,
    k_weight,
    v_weight,
    out_weight,
    q_gain,
    k_gain,
    out_ref,
    gathered,
    normed,
    w_all,
    w_out,
    raw,
    heads_q,
    heads_k,
    heads_v,
    attended,
    partial,
    got_full,
    got_half,
    stat_own,
    stat_got,
    columns,
    mod_sum,
    mod_got_a,
    mod_got_b,
    mod_got_c,
    mod_total,
    send_sems,
    recv_sems,
    mod_send,
    mod_recv,
    load_sems,
):
    clips, rows = stream_in.shape[0], stream_in.shape[1]
    width = stream_in.shape[2]
    local_cols = q_weight.shape[2]
    local_heads = local_cols // HEAD
    tokens = rows * CTX
    mod_cols = mod_part.shape[1] // CTX
    lanes_pipe = min(4, pipe_count)
    depth_pipe = pipe_count // lanes_pipe

    pipe = lax.axis_index("pipe")
    ctx = lax.axis_index("ctx")
    y, side = ctx // 2, ctx % 2

    def at_ctx(row, col):
        return lax.rem(row + 4, 4) * 2 + col

    c_up, c_down, c_far = at_ctx(y + 1, side), at_ctx(y - 1, side), at_ctx(y + 2, side)
    c_pair = at_ctx(y, 1 - side)
    c_pair_up, c_pair_down, c_pair_far = (
        at_ctx(y + 1, 1 - side),
        at_ctx(y - 1, 1 - side),
        at_ctx(y + 2, 1 - side),
    )
    up, down, pair = (pipe, c_up), (pipe, c_down), (pipe, c_pair)

    core = lax.rem(pipe, 2)
    if pipe_count >= 4:
        z = lax.rem(pipe // 2, depth_pipe)
        x_lo = pipe // (2 * depth_pipe)

        def depth_peer(step):
            return ((x_lo * depth_pipe + lax.rem(z + step, depth_pipe)) * 2 + core, ctx)

        def quad_peer(step):
            there = lax.rem(x_lo * 2 + core + step, 4)
            return (((there // 2) * depth_pipe + z) * 2 + lax.rem(there, 2), ctx)

    else:

        def depth_peer(step):
            return (pipe, ctx)

        def quad_peer(step):
            return (lax.rem(pipe + step, lanes_pipe), ctx)

    def ctx_peer(step):
        return (pipe, lax.rem(ctx + step, CTX))

    after = (lax.rem(pipe + 1, pipe_count), ctx)
    before = (lax.rem(pipe + pipe_count - 1, pipe_count), ctx)

    loads = [
        pltpu.make_async_copy(
            stream_in.at[m], gathered.at[m, pl.ds(pl.multiple_of(ctx * rows, rows), rows)], load_sems.at[m]
        )
        for m in range(clips)
    ]
    weights = [
        pltpu.make_async_copy(w.at[0], w_all.at[:, pl.ds(i * local_cols, local_cols)], load_sems.at[clips + i])
        for i, w in enumerate((q_weight, k_weight, v_weight))
    ] + [pltpu.make_async_copy(out_weight.at[0], w_out, load_sems.at[clips + 3])]
    for copy in loads:
        copy.start()

    greeted = (
        [ctx_peer(s) for s in range(1, CTX)]
        + [depth_peer(s) for s in range(1, depth_pipe)]
        + [quad_peer(s) for s in range(1, lanes_pipe)]
        + [after, before]
    )
    barrier = pltpu.get_barrier_semaphore()
    for peer in greeted:
        pl.semaphore_signal(barrier, inc=1, device_id=peer, device_id_type=MESH)
    pl.semaphore_wait(barrier, len(greeted))

    def remote(src, dst, number, peer, sends=send_sems, recvs=recv_sems):
        return pltpu.make_async_remote_copy(
            src_ref=src,
            dst_ref=dst,
            send_sem=sends.at[number],
            recv_sem=recvs.at[number],
            device_id=peer,
            device_id_type=MESH,
        )

    def block(ref, m, owner, first=0, count=rows):
        return ref.at[m, pl.ds(pl.multiple_of(owner * rows + first, 16), count)]

    half = rows // 2

    class Gather:
        def __init__(self, m):
            base = m * PER_CLIP + GATHER

            def send(owner, number, peer, first=0, count=rows):
                part = block(gathered, m, owner, first, count)
                return remote(part, part, base + number, peer)

            self.own = [send(ctx, 0, up), send(ctx, 1, down), send(ctx, 2, pair)]
            self.far_halves = [send(c_down, 3, up, 0, half), send(c_up, 4, down, half, half)]
            self.others = [send(c_pair, 5, up), send(c_pair, 6, down)]
            self.far_pair = [send(c_far, 7, pair)]
            self.all = self.own + self.far_halves + self.others + self.far_pair

        def start_own(self):
            for copy in self.own:
                copy.start()

        def forward_near(self):
            self.own[0].wait_recv()
            self.far_halves[0].start()
            self.own[1].wait_recv()
            self.far_halves[1].start()
            self.own[2].wait_recv()
            for copy in self.others:
                copy.start()

        def forward_far(self):
            for copy in self.far_halves:
                copy.wait_recv()
            self.far_pair[0].start()

        def finish(self):
            for copy in self.others + self.far_pair:
                copy.wait_recv()

        def drain(self):
            for copy in self.all:
                copy.wait_send()

    gathers = [Gather(m) for m in range(clips)]

    def add_into(m, owner, first, count, sources):
        def step(i, carry):
            at = pl.ds(pl.multiple_of(owner * rows + first + i * CHUNK, CHUNK), CHUNK)
            total = partial[m, at].astype(jnp.float32)
            for source in sources:
                total = total + source[pl.ds(i * CHUNK, CHUNK)].astype(jnp.float32)
            partial[m, at] = total.astype(jnp.bfloat16)
            return carry

        lax.fori_loop(0, count // CHUNK, step, 0)

    class Reduce:
        def __init__(self, m):
            self.m = m
            base = m * PER_CLIP + REDUCE
            full = [got_full.at[m, i] for i in range(6)]
            halves = [got_half.at[m, i] for i in range(2)]
            self.full, self.halves = full, halves

            def send(owner, number, peer, into, first=0, count=rows):
                return remote(block(partial, m, owner, first, count), into, base + number, peer)

            self.far_pair = send(c_pair_far, 0, pair, full[0])
            self.other_up = send(c_pair_up, 1, up, full[1])
            self.other_down = send(c_pair_down, 2, down, full[2])
            self.far_down = send(c_far, 3, down, halves[0], 0, half)
            self.far_up = send(c_far, 4, up, halves[1], half, half)
            self.near_down = send(c_down, 5, down, full[3])
            self.near_up = send(c_up, 6, up, full[4])
            self.pair = send(c_pair, 7, pair, full[5])
            self.all = [
                self.far_pair,
                self.other_up,
                self.other_down,
                self.far_down,
                self.far_up,
                self.near_down,
                self.near_up,
                self.pair,
            ]

        def start(self):
            self.far_pair.start()
            self.other_up.start()
            self.other_down.start()

        def second(self):
            self.far_pair.wait_recv()
            add_into(self.m, c_far, 0, rows, [self.full[0]])
            self.far_down.start()
            self.far_up.start()
            self.other_up.wait_recv()
            self.other_down.wait_recv()
            add_into(self.m, c_pair, 0, rows, [self.full[1], self.full[2]])
            self.pair.start()

        def third(self):
            self.far_down.wait_recv()
            add_into(self.m, c_down, 0, half, [self.halves[0]])
            self.near_down.start()
            self.far_up.wait_recv()
            add_into(self.m, c_up, half, half, [self.halves[1]])
            self.near_up.start()

        def last(self):
            self.near_down.wait_recv()
            self.near_up.wait_recv()
            self.pair.wait_recv()
            m = self.m
            gate = mod_total[pl.ds(m, 1), 2 * width : 3 * width] + layer_row[:, 2 * width : 3 * width]

            def step(i, carry):
                at = pl.ds(pl.multiple_of(ctx * rows + i * CHUNK, CHUNK), CHUNK)
                here = pl.ds(i * CHUNK, CHUNK)
                branch = partial[m, at].astype(jnp.float32)
                for source in self.full[3:]:
                    branch = branch + source[here].astype(jnp.float32)
                result = gathered[m, at].astype(jnp.float32) + gate * branch
                partial[m, at] = result.astype(jnp.bfloat16)
                return carry

            lax.fori_loop(0, rows // CHUNK, step, 0)

        def drain(self):
            for copy in self.all:
                copy.wait_send()

    reduces = [Reduce(m) for m in range(clips)]
    hands = [
        remote(block(partial, m, ctx), out_ref.at[m], m * PER_CLIP + HAND, after) for m in range(clips)
    ]

    def hand_off(m):
        @pl.when(pipe < pipe_count - 1)
        def _():
            hands[m].start()

    def norm_block(m, owner):
        shift = mod_total[pl.ds(m, 1), 0:width] + layer_row[:, 0:width]
        scale = 1.0 + (mod_total[pl.ds(m, 1), width : 2 * width] + layer_row[:, width : 2 * width])

        def step(i, carry):
            at = pl.ds(pl.multiple_of(owner * rows + i * CHUNK, CHUNK), CHUNK)
            values = gathered[m, at].astype(jnp.float32)
            center = values - jnp.mean(values, -1, keepdims=True)
            spread = jnp.mean(center * center, -1, keepdims=True)
            normed[m, at] = (center * lax.rsqrt(spread + 1e-06) * scale + shift).astype(jnp.bfloat16)
            return carry

        lax.fori_loop(0, rows // CHUNK, step, 0)

    def project(m):
        def step(i, carry):
            cols = pl.ds(pl.multiple_of(i * local_cols, local_cols), local_cols)
            raw[:, cols] = jnp.dot(normed[m], w_all[:, cols], preferred_element_type=jnp.float32)
            return carry

        lax.fori_loop(0, 3, step, 0)

    stat_sends = [
        [
            remote(stat_own.at[m], stat_got.at[m, s - 1], m * PER_CLIP + STATS + s - 1, ctx_peer(s))
            for s in range(1, CTX)
        ]
        for m in range(clips)
    ]

    def start_stats(m):
        q_raw = raw[:, 0:local_cols]
        k_raw = raw[:, local_cols : 2 * local_cols]
        q_sum = jnp.sum(q_raw * q_raw, -1, keepdims=True)
        k_sum = jnp.sum(k_raw * k_raw, -1, keepdims=True)
        lane = lax.broadcasted_iota(jnp.int32, (tokens, HEAD), 1)
        both = jnp.where(lane == 0, q_sum, k_sum)
        stat_own[m] = both.T[0:2]
        for copy in stat_sends[m]:
            copy.start()

    def finish_stats(m):
        total = stat_own[m]
        for s, copy in enumerate(stat_sends[m]):
            copy.wait_recv()
            total = total + stat_got[m, s]
        inverse = lax.rsqrt(total / width + 1e-06)
        columns[...] = jnp.concatenate([inverse, jnp.zeros((HEAD - 2, tokens), jnp.float32)], 0).T

    def rope(m):
        def step(h, carry):
            for kind, (gain, target) in enumerate(((q_gain, heads_q), (k_gain, heads_k))):
                here = pl.ds(pl.multiple_of(h * HEAD, HEAD), HEAD)
                there = pl.ds(pl.multiple_of(kind * local_cols + h * HEAD, HEAD), HEAD)
                value = raw[:, there] * columns[:, kind : kind + 1] * gain[:, here]
                turned = value * cos_ref[...] + pltpu.roll(value, HEAD // 2, 1) * sin_ref[...]
                target[:, here] = turned.astype(jnp.bfloat16)
            return carry

        lax.fori_loop(0, local_heads, step, 0)
        heads_v[...] = raw[:, 2 * local_cols : 3 * local_cols].astype(jnp.bfloat16)

    q_rows = 256

    def attend(m):
        def step(i, carry):
            h, r = i // (tokens // q_rows), lax.rem(i, tokens // q_rows)
            here = pl.ds(pl.multiple_of(h * HEAD, HEAD), HEAD)
            at = pl.ds(pl.multiple_of(r * q_rows, q_rows), q_rows)
            scores = lax.dot_general(
                heads_q[at, here], heads_k[:, here], (((1,), (1,)), ((), ())), preferred_element_type=jnp.float32
            ) * HEAD ** (-0.5)
            scores = scores - jnp.max(scores, -1, keepdims=True)
            weights = jnp.exp(scores)
            total = jnp.sum(weights, -1, keepdims=True)
            mixed = jnp.dot(weights.astype(jnp.bfloat16), heads_v[:, here], preferred_element_type=jnp.float32)
            attended[at, here] = (mixed / total).astype(jnp.bfloat16)
            return carry

        lax.fori_loop(0, local_heads * (tokens // q_rows), step, 0)

    out_cols = 512

    def project_out(m):
        def step(i, carry):
            cols = pl.ds(pl.multiple_of(i * out_cols, out_cols), out_cols)
            partial[m, :, cols] = jnp.dot(
                attended[...], w_out[:, cols], preferred_element_type=jnp.float32
            ).astype(jnp.bfloat16)
            return carry

        lax.fori_loop(0, width // out_cols, step, 0)

    def mod_slice(ref, index):
        return ref.at[:, pl.ds(pl.multiple_of(index * mod_cols, 128), mod_cols)]

    mod_a = [
        remote(
            mod_slice(mod_part, lax.rem(ctx + s, CTX)), mod_got_a.at[s - 1], s - 1, ctx_peer(s), mod_send, mod_recv
        )
        for s in range(1, CTX)
    ]
    number = CTX - 1
    mod_b = [
        remote(mod_sum.at[0], mod_got_b.at[s - 1], number + s - 1, depth_peer(s), mod_send, mod_recv)
        for s in range(1, depth_pipe)
    ]
    number += depth_pipe - 1
    mod_c = [
        remote(mod_sum.at[1], mod_got_c.at[s - 1], number + s - 1, quad_peer(s), mod_send, mod_recv)
        for s in range(1, lanes_pipe)
    ]
    number += lanes_pipe - 1
    mod_d = [
        remote(mod_slice(mod_total, ctx), mod_slice(mod_total, ctx), number + s - 1, ctx_peer(s), mod_send, mod_recv)
        for s in range(1, CTX)
    ]
    own_cols = pl.ds(pl.multiple_of(ctx * mod_cols, 128), mod_cols)

    def summed(value, copies, got):
        for i, copy in enumerate(copies):
            copy.wait_recv()
            value = value + got[i]
        return value

    for copy in mod_a:
        copy.start()
    for copy in loads:
        copy.wait()
    gathers[0].start_own()
    for copy in weights:
        copy.start()
    mod_sum[0] = summed(mod_part[:, own_cols], mod_a, mod_got_a)
    for copy in mod_b:
        copy.start()
    mod_sum[1] = summed(mod_sum[0], mod_b, mod_got_b)
    for copy in mod_c:
        copy.start()
    mod_total[:, own_cols] = summed(mod_sum[1], mod_c, mod_got_c)
    for copy in mod_d:
        copy.start()
    gathers[0].forward_near()
    for copy in mod_d:
        copy.wait_recv()
    for owner in (ctx, c_up, c_down, c_pair):
        norm_block(0, owner)
    gathers[0].forward_far()
    gathers[1].start_own()
    norm_block(0, c_far)
    for copy in weights:
        copy.wait()
    gathers[0].finish()
    for owner in (c_pair_up, c_pair_down, c_pair_far):
        norm_block(0, owner)
    project(0)
    start_stats(0)
    gathers[1].forward_near()
    for owner in (ctx, c_up, c_down, c_pair):
        norm_block(1, owner)
    finish_stats(0)
    rope(0)
    gathers[1].forward_far()
    attend(0)
    project_out(0)
    reduces[0].start()
    norm_block(1, c_far)
    gathers[1].finish()
    for owner in (c_pair_up, c_pair_down, c_pair_far):
        norm_block(1, owner)
    project(1)
    start_stats(1)
    reduces[0].second()
    finish_stats(1)
    rope(1)
    reduces[0].third()
    attend(1)
    project_out(1)
    reduces[1].start()
    reduces[0].last()
    hand_off(0)
    reduces[1].second()
    reduces[1].third()
    reduces[1].last()
    hand_off(1)

    for gather in gathers:
        gather.drain()
    for reduce in reduces:
        reduce.drain()
    for copy in mod_a + mod_b + mod_c + mod_d:
        copy.wait_send()
    for sends in stat_sends:
        for copy in sends:
            copy.wait_send()

    @pl.when(pipe < pipe_count - 1)
    def _():
        for copy in hands:
            copy.wait_send()

    @pl.when(pipe > 0)
    def _():
        for copy in hands:
            copy.wait_recv()

    @pl.when(pipe == 0)
    def _():
        out_ref[...] = jnp.zeros_like(out_ref)


def shards(
    inflow,
    patches,
    patch_weight,
    timesteps,
    time_weight,
    mod_weight,
    layer_table,
    section_layer,
    token_cell,
    q_weight,
    k_weight,
    v_weight,
    out_weight,
    q_gain,
    k_gain,
):
    clips, rows, width = inflow.shape[1:]
    local_cols = q_weight.shape[2]
    tokens = rows * CTX
    pipe_count = lax.axis_size("pipe")
    section = lax.axis_index("pipe")
    time_hidden = jax.nn.silu(
        jnp.dot(
            time_features(timesteps, time_weight.shape[0]),
            time_weight,
            preferred_element_type=jnp.float32,
        )
    ).astype(jnp.bfloat16)
    share_rows = mod_weight.shape[0]
    flat_rank = lax.axis_index(("pipe", "ctx"))
    time_piece = lax.dynamic_slice_in_dim(time_hidden, flat_rank * share_rows, share_rows, 1)
    mod_part = jnp.dot(time_piece, mod_weight, preferred_element_type=jnp.float32)
    section_ids = jnp.arange(section_layer.shape[0], dtype=jnp.int32)
    layer_id = jnp.sum(jnp.where(section_ids == section, section_layer, 0))
    layer_row = jnp.sum(
        jnp.where((section_ids == layer_id)[:, None], layer_table.astype(jnp.float32), 0.0), 0, keepdims=True
    )
    embedded = jnp.einsum(
        "btp,pd->btd", patches, patch_weight, preferred_element_type=jnp.float32
    ).astype(jnp.bfloat16)
    start_block = jnp.where(section == 0, embedded, inflow[0])
    cos_table, sin_table = rope_tables(token_cell)

    vmem = pl.BlockSpec(memory_space=pltpu.VMEM)
    anywhere = pl.BlockSpec(memory_space=pl.ANY)
    mod_width = layer_row.shape[1]
    mod_cols = mod_width // CTX
    lanes_pipe = min(4, pipe_count)
    depth_pipe = pipe_count // lanes_pipe
    mod_copies = 2 * (CTX - 1) + depth_pipe - 1 + lanes_pipe - 1
    bf16, f32 = jnp.bfloat16, jnp.float32
    handed = pl.pallas_call(
        functools.partial(section_kernel, pipe_count),
        out_shape=jax.ShapeDtypeStruct((clips, rows, width), bf16),
        in_specs=[anywhere, vmem, vmem, vmem, vmem, anywhere, anywhere, anywhere, anywhere, vmem, vmem],
        out_specs=vmem,
        scratch_shapes=[
            pltpu.VMEM((clips, tokens, width), bf16),
            pltpu.VMEM((clips, tokens, width), bf16),
            pltpu.VMEM((width, 3 * local_cols), bf16),
            pltpu.VMEM((local_cols, width), bf16),
            pltpu.VMEM((tokens, 3 * local_cols), f32),
            pltpu.VMEM((tokens, local_cols), bf16),
            pltpu.VMEM((tokens, local_cols), bf16),
            pltpu.VMEM((tokens, local_cols), bf16),
            pltpu.VMEM((tokens, local_cols), bf16),
            pltpu.VMEM((clips, tokens, width), bf16),
            pltpu.VMEM((clips, 6, rows, width), bf16),
            pltpu.VMEM((clips, 2, rows // 2, width), bf16),
            pltpu.VMEM((clips, 2, tokens), f32),
            pltpu.VMEM((clips, CTX - 1, 2, tokens), f32),
            pltpu.VMEM((tokens, HEAD), f32),
            pltpu.VMEM((2, clips, mod_cols), f32),
            pltpu.VMEM((CTX - 1, clips, mod_cols), f32),
            pltpu.VMEM((max(depth_pipe - 1, 1), clips, mod_cols), f32),
            pltpu.VMEM((max(lanes_pipe - 1, 1), clips, mod_cols), f32),
            pltpu.VMEM((clips, mod_width), f32),
            pltpu.SemaphoreType.DMA((clips * PER_CLIP,)),
            pltpu.SemaphoreType.DMA((clips * PER_CLIP,)),
            pltpu.SemaphoreType.DMA((mod_copies,)),
            pltpu.SemaphoreType.DMA((mod_copies,)),
            pltpu.SemaphoreType.DMA((clips + 4,)),
        ],
        compiler_params=pltpu.CompilerParams(
            collective_id=0, has_side_effects=True, vmem_limit_bytes=56 * 2**20
        ),
        cost_estimate=pl.CostEstimate(
            flops=2 * clips * tokens * width * local_cols * 4, bytes_accessed=4 * width * local_cols * 2, transcendentals=0
        ),
    )(
        start_block,
        mod_part,
        layer_row,
        cos_table,
        sin_table,
        q_weight,
        k_weight,
        v_weight,
        out_weight,
        q_gain,
        k_gain,
    )
    return handed[None]


def solution(mesh):
    placed = (
        P("pipe", None, "ctx", None),
        P(None, "ctx", None),
        P(),
        P(),
        P(),
        P(("pipe", "ctx"), None),
        P(),
        P(),
        P(),
        P("pipe", None, "ctx"),
        P("pipe", None, "ctx"),
        P("pipe", None, "ctx"),
        P("pipe", "ctx", None),
        P("pipe", "ctx"),
        P("pipe", "ctx"),
    )
    return jax.shard_map(
        shards, mesh=mesh, in_specs=placed, out_specs=P("pipe", None, "ctx", None), check_vma=False
    )
```

time: 555 us -> 133 us (0.24)
  waiting for transfers between devices: 416 us -> 0 us
  Pallas kernels: 0 us -> 121 us
  matrix products: 39.7 us -> 2.44 us
  local copies, waits for them, and re-layouts: 26.4 us -> 2.09 us
  other arithmetic: 28.9 us -> 7.18 us
  blocking collectives: 17.6 us -> 0 us
  between operations: 15.4 us -> 0.08 us
  starting transfers between devices: 5.55 us -> 0 us
    psum x1 -> x0, waiting for transfers between devices: 256 us -> none  [shards(): lax.psum(jnp.dot(time_piece, mod_weight, preferred_element_type=jnp.float...]
    reduce_scatter x2 -> x0, waiting for transfers between devices: 150 us -> none  [shards(): lax.psum_scatter(jnp.dot(attended, w_out, preferred_element_type=jnp.floa...]
    pallas_call x0 -> x1, Pallas kernels: none -> 121 us  [shards(): pl.pallas_call(functools.partial(section_kernel, pipe_count), out_shape=j...]
    dot_general x12 -> x0, matrix products: 34.5 us -> none  [the longest x2 9.84 us: one_block(): jnp.einsum('hts,shd->thd', probs, val_heads, preferred_element_type=jnp.f...]
    unnamed x47 -> x13, local copies, waits for them, and re-layouts: 21.7 us -> 2.09 us
    psum x1 -> x0, blocking collectives: 17.6 us -> none  [shards(): lax.psum((jnp.sum(q_raw * q_raw, -1), jnp.sum(k_raw * k_raw, -1)), 'ctx')]
    ppermute x1 -> x0, waiting for transfers between devices: 8.91 us -> none  [passed_along(): lax.ppermute(value, axis, [(source, source + steps) for source in range(f...]
    reduce_sum x4 -> x0, other arithmetic: 6.96 us -> none  [the longest x2 5.05 us: modulated_norm(): center = values_f - jnp.mean(values_f, -1, keepdims=True)]
  transfers between devices with their start and end apart: 6 -> 0, of which waited for: 4 -> 0; matrix products, arithmetic and copies ran while one was open for 5% -> 0% of each run, Pallas kernels for 0% -> 0%
where the time goes in v1:
time: 133 us
  Pallas kernels  121 us (91%)
  other arithmetic  7.18 us (5%)
  matrix products  2.44 us (2%)
  local copies, waits for them, and re-layouts  2.09 us (2%)
    pallas_call x1, Pallas kernels, shards(): pl.pallas_call(functools.partial(section_kernel, pipe_count), out_shape=j...  121 us

profile of v1, /device:TPU:5, one launch (start us, length us, event | category | flops | bytes accessed | tf_op | source)
XLA Modules:
  0.0 133.2 jit_solution(12078422282348578408)
XLA Ops:
  0.0 0.0 copy-start
  0.0 0.0 copy-start.2
  0.0 0.0 copy-start.4
  0.0 1.4 %fusion.16 = s32[]{:T(128)} fusion(s32[32]{0:T(128)} %param.22, s32[]{:T(128)S(6)} %axis_index.27), kind=kLoop, calls=%fused_computation.37 | loop fusion | flops 95 | bytes 136 | tf_op jit(solution)/shard_map/reduce_sum | solution.py:572
  1.5 0.6 iota_compare_fusion.2
  2.1 0.7 convert_element_type.24
  2.8 0.1 fusion.7
  2.9 0.7 add_select_fusion.3
  3.6 0.0 copy-done
  3.7 0.3 fusion.9
  4.0 0.0 copy-done.2
  4.0 0.0 copy-start.1
  4.0 0.0 copy-start.3
  4.0 0.0 copy-start.5
  4.0 0.9 select_reduce_fusion
  4.8 0.0 copy-done.4
  4.9 0.9 fusion.14.mod_part
  5.7 1.7 %fusion.4 = (f32[512,64]{1,0:T(8,128)S(1)}, f32[512,64]{1,0:T(8,128)S(1)}, f32[512,64]{1,0:T(8,128)S(1)}) fusion(f32[64]{0:T(128)S(1)} %negate_power_fusion, s32[512]{0:T(512)S(1)} %get-tuple-element.9, s32[512]{0:T(512)S(1)} %get-tuple-element.10, pred[64]{0:T(512)(128)(4,1)S(1)} %iota_compare_fusion, s32[512]{0:T(512)S(1)} %get-tuple-element.8, ...), kind=kLoop, calls=%fused_computation.9 | loop fusion | flops 163840 | bytes 399744 | tf_op jit(solution)/shard_map/neg | solution.py:56
  7.5 1.0 pad_maximum_fusion
  8.5 0.0 copy-done.1
  8.5 0.0 copy-done.3
  8.5 0.0 copy-done.5
  8.5 1.2 fusion.stream_in
  9.7 121.4 %shard_map.145 = bf16[2,64,3072]{2,1,0:T(8,128)(2,1)} custom-call(bf16[2,64,3072]{2,1,0:T(8,128)(2,1)} %fusion.stream_in, f32[2,9216]{1,0:T(2,128)} %fusion.14.mod_part, f32[1,9216]{1,0:T(1,128)} %bitcast.11, f32[512,128]{1,0:T(8,128)} %get-tuple-element.13.cos_ref, f32[512,128]{1,0:T(8,128)} %get-tuple-element.14.sin_ref, bf16[1,3072,384]{2,1,0:T(8,128)(2,1)} %q_weight.1, ...), custom_call_target="tpu_custom_call" | custom-call | flops 9663676416 | bytes 9437184 | tf_op jit(solution)/shard_map/pallas_call | solution.py:590
  131.1 2.1 %copy.17 = bf16[1,2,64,3072]{3,2,1,0:T(8,128)(2,1)} copy(bf16[1,2,64,3072]{3,2,1,0:T(8,128)(2,1)} %bitcast.10) | data formatting | bytes 1572864
  (4 shorter events, 0.0 us)
Async XLA Ops:
  0.0 3.6 %copy-start = (bf16[256,3072]{1,0:T(8,128)(2,1)S(1)}, bf16[256,3072]{1,0:T(8,128)(2,1)}, u32[]{:S(2)}) copy-start(bf16[256,3072]{1,0:T(8,128)(2,1)} %param.19) | copy-start | bytes 4718596
  0.0 4.0 %copy-start.2 = (bf16[32,9216]{1,0:T(8,128)(2,1)S(1)}, bf16[32,9216]{1,0:T(8,128)(2,1)}, u32[]{:S(2)}) copy-start(bf16[32,9216]{1,0:T(8,128)(2,1)} %param.21) | copy-start | bytes 1769476
  0.0 4.8 %copy-start.4 = (bf16[12,9216]{1,0:T(8,128)(2,1)S(1)}, bf16[12,9216]{1,0:T(8,128)(2,1)}, u32[]{:S(2)}) copy-start(bf16[12,9216]{1,0:T(8,128)(2,1)} %param.20) | copy-start | bytes 663556
  4.0 4.5 %copy-start.1 = (bf16[1,2,64,3072]{3,2,1,0:T(8,128)(2,1)S(1)}, bf16[1,2,64,3072]{3,2,1,0:T(8,128)(2,1)}, u32[]{:S(2)}) copy-start(bf16[1,2,64,3072]{3,2,1,0:T(8,128)(2,1)} %param.15) | copy-start | bytes 2359300
  4.0 4.5 %copy-start.3 = (bf16[64,3072]{1,0:T(8,128)(2,1)S(1)}, bf16[64,3072]{1,0:T(8,128)(2,1)}, u32[]{:S(2)}) copy-start(bf16[64,3072]{1,0:T(8,128)(2,1)} %param.17) | copy-start | bytes 1179652
  4.0 4.5 %copy-start.5 = (bf16[2,64,64]{2,1,0:T(8,128)(2,1)S(1)}, bf16[2,64,64]{2,1,0:T(8,128)(2,1)}, u32[]{:S(2)}) copy-start(bf16[2,64,64]{2,1,0:T(8,128)(2,1)} %param.16) | copy-start | bytes 49156

commit v2 on v1

v2 whole, which is shorter than its diff:
```python
import functools

import jax
import jax.numpy as jnp
import numpy as np
from jax import lax
from jax.experimental import pallas as pl
from jax.experimental.pallas import tpu as pltpu
from jax.sharding import PartitionSpec as P

HEAD = 128
GRID_H = 8
GRID_W = 16
MESH = pl.DeviceIdType.MESH
CTX = 8
CHUNK = 16
SPACE_PAIRS = HEAD // 6
TIME_PAIRS = HEAD // 2 - 2 * SPACE_PAIRS

GATHER_PARTS = (2, 2)
REDUCE_PARTS = (2, 3)
PARTS = 3
GATHER = 0
REDUCE = 10
PER_PART = 21
STATS = CTX - 1


def column_parts(width, parts):
    span = width // parts
    cross = span // 6 // 128 * 128
    return [
        (slice(p * span, (p + 1) * span), slice(p * span, (p + 1) * span - cross), slice((p + 1) * span - cross, (p + 1) * span))
        for p in range(parts)
    ]


def rate_rows(freq_count):
    half_freq = freq_count // 2
    time_rates = 10000.0 ** (-np.arange(half_freq) / half_freq)
    half_size = HEAD // 2
    pair_ids = np.arange(half_size)
    exponent = np.where(
        pair_ids < TIME_PAIRS,
        pair_ids / TIME_PAIRS,
        np.where(
            pair_ids < TIME_PAIRS + SPACE_PAIRS,
            (pair_ids - TIME_PAIRS) / SPACE_PAIRS,
            (pair_ids - TIME_PAIRS - SPACE_PAIRS) / SPACE_PAIRS,
        ),
    )
    table = np.zeros((8, max(freq_count, HEAD)), np.float32)
    table[0, :freq_count] = np.concatenate([time_rates, time_rates])
    table[1, :HEAD] = np.concatenate([10000.0 ** (-exponent)] * 2)
    return table


def section_kernel(
    pipe_count,
    timesteps,
    section_layer,
    inflow,
    patches,
    patch_weight,
    time_weight,
    mod_weight,
    layer_table,
    token_cell,
    rates,
    q_weight,
    k_weight,
    v_weight,
    out_weight,
    q_gain,
    k_gain,
    out_ref,
    gathered,
    normed,
    w_all,
    w_out,
    raw,
    heads_q,
    heads_k,
    heads_v,
    attended,
    partial,
    got_full,
    got_half,
    got_cross,
    stat_own,
    stat_got,
    columns,
    mod_sum,
    mod_got_a,
    mod_got_b,
    mod_got_c,
    mod_total,
    mod_part,
    modulation,
    cos_ref,
    sin_ref,
    w_time,
    w_patch,
    w_layer,
    patch_rows,
    send_sems,
    recv_sems,
    mod_send,
    mod_recv,
    load_sems,
):
    clips, rows, width = inflow.shape[1:]
    local_cols = q_weight.shape[2]
    local_heads = local_cols // HEAD
    tokens = rows * CTX
    mod_cols = mod_part.shape[1] // CTX
    lanes_pipe = min(4, pipe_count)
    depth_pipe = pipe_count // lanes_pipe

    pipe = lax.axis_index("pipe")
    ctx = lax.axis_index("ctx")
    y, side = ctx // 2, ctx % 2

    def at_ctx(row, col):
        return lax.rem(row + 4, 4) * 2 + col

    c_up, c_down, c_far = at_ctx(y + 1, side), at_ctx(y - 1, side), at_ctx(y + 2, side)
    c_pair = at_ctx(y, 1 - side)
    c_pair_up, c_pair_down, c_pair_far = (
        at_ctx(y + 1, 1 - side),
        at_ctx(y - 1, 1 - side),
        at_ctx(y + 2, 1 - side),
    )
    up, down, pair = (pipe, c_up), (pipe, c_down), (pipe, c_pair)

    core = lax.rem(pipe, 2)
    if pipe_count >= 4:
        z = lax.rem(pipe // 2, depth_pipe)
        x_lo = pipe // (2 * depth_pipe)

        def depth_peer(step):
            return ((x_lo * depth_pipe + lax.rem(z + step, depth_pipe)) * 2 + core, ctx)

        def quad_peer(step):
            there = lax.rem(x_lo * 2 + core + step, 4)
            return (((there // 2) * depth_pipe + z) * 2 + lax.rem(there, 2), ctx)

    else:

        def depth_peer(step):
            return (pipe, ctx)

        def quad_peer(step):
            return (lax.rem(pipe + step, lanes_pipe), ctx)

    def ctx_peer(step):
        return (pipe, lax.rem(ctx + step, CTX))

    after = (lax.rem(pipe + 1, pipe_count), ctx)
    before = (lax.rem(pipe + pipe_count - 1, pipe_count), ctx)

    def own_rows(m):
        return gathered.at[m, pl.ds(pl.multiple_of(ctx * rows, rows), rows)]

    loads = [pltpu.make_async_copy(inflow.at[0, m], own_rows(m), load_sems.at[m]) for m in range(clips)]
    share = mod_weight.shape[0]
    time_cols = w_time.shape[1]
    shares = time_cols // share
    rank = pipe * CTX + ctx
    time_load = pltpu.make_async_copy(
        time_weight.at[:, pl.ds(pl.multiple_of((rank // shares) * time_cols, 128), time_cols)],
        w_time,
        load_sems.at[clips],
    )
    layer_load = pltpu.make_async_copy(layer_table, w_layer, load_sems.at[clips + 1])
    patch_loads = [
        pltpu.make_async_copy(patch_weight, w_patch, load_sems.at[clips + 2]),
        pltpu.make_async_copy(patches, patch_rows, load_sems.at[clips + 3]),
    ]
    weights = [
        pltpu.make_async_copy(w.at[0], w_all.at[:, pl.ds(i * local_cols, local_cols)], load_sems.at[clips + 4 + i])
        for i, w in enumerate((q_weight, k_weight, v_weight))
    ] + [pltpu.make_async_copy(out_weight.at[0], w_out, load_sems.at[clips + 7])]

    @pl.when(pipe > 0)
    def _():
        for copy in loads:
            copy.start()

    @pl.when(pipe == 0)
    def _():
        for copy in patch_loads:
            copy.start()

    time_load.start()
    layer_load.start()

    greeted = (
        [ctx_peer(s) for s in range(1, CTX)]
        + [depth_peer(s) for s in range(1, depth_pipe)]
        + [quad_peer(s) for s in range(1, lanes_pipe)]
        + [after, before]
    )
    barrier = pltpu.get_barrier_semaphore()
    for peer in greeted:
        pl.semaphore_signal(barrier, inc=1, device_id=peer, device_id_type=MESH)

    lane = lax.broadcasted_iota(jnp.int32, (8, rates.shape[1]), 1)
    line = lax.broadcasted_iota(jnp.int32, (8, rates.shape[1]), 0)
    steps = jnp.where(line == 0, timesteps[0], timesteps[1]).astype(jnp.float32)
    angles = steps * rates[0:1, :]
    features = jnp.where(lane < rates.shape[1] // 2, jnp.cos(angles), jnp.sin(angles)).astype(jnp.bfloat16)
    time_load.wait()
    time_hidden = jax.nn.silu(
        jnp.dot(features, w_time[...], preferred_element_type=jnp.float32)
    ).astype(jnp.bfloat16)
    first = lax.rem(rank, shares) * share
    picked = lax.broadcasted_iota(jnp.int32, (time_cols, 128), 0) - first
    picks = (picked == lax.broadcasted_iota(jnp.int32, (time_cols, 128), 1)).astype(jnp.bfloat16)
    time_piece = jnp.dot(time_hidden, picks, preferred_element_type=jnp.float32).astype(jnp.bfloat16)
    mod_part[...] = jnp.dot(
        time_piece[:, :share], mod_weight[...], preferred_element_type=jnp.float32
    )[:clips]

    @pl.when(pipe == 0)
    def _():
        for copy in patch_loads:
            copy.wait()
        for m in range(clips):
            embedded = jnp.dot(patch_rows[m], w_patch[...], preferred_element_type=jnp.float32)
            gathered[m, pl.ds(pl.multiple_of(ctx * rows, rows), rows)] = embedded.astype(jnp.bfloat16)

    @pl.when(pipe > 0)
    def _():
        for copy in loads:
            copy.wait()

    pl.semaphore_wait(barrier, len(greeted))

    def remote(src, dst, number, peer, sends=send_sems, recvs=recv_sems):
        return pltpu.make_async_remote_copy(
            src_ref=src,
            dst_ref=dst,
            send_sem=sends.at[number],
            recv_sem=recvs.at[number],
            device_id=peer,
            device_id_type=MESH,
        )

    def block(ref, m, owner, first=0, count=rows, cols=slice(None)):
        return ref.at[m, pl.ds(pl.multiple_of(owner * rows + first, 16), count), cols]

    half = rows // 2

    class Gather:
        def __init__(self, m, part, columns_of):
            base = (m * PARTS + part) * PER_PART + GATHER
            whole, straight, crossing = columns_of

            def send(owner, number, peer, first=0, count=rows, cols=whole):
                piece = block(gathered if m == 0 else normed, m, owner, first, count, cols)
                return remote(piece, piece, base + number, peer)

            self.own = [send(ctx, 0, up), send(ctx, 1, down), send(ctx, 2, pair)]
            self.far_up = send(c_down, 3, up, 0, half)
            self.far_down = send(c_up, 4, down, half, half)
            self.other_up = send(c_pair, 5, up, cols=straight)
            self.other_down = send(c_pair, 6, down, cols=straight)
            self.far_pair = send(c_far, 7, pair)
            self.cross_up = send(c_down, 8, pair, cols=crossing)
            self.cross_down = send(c_up, 9, pair, cols=crossing)
            self.rest = [self.other_up, self.other_down, self.cross_up, self.cross_down, self.far_pair]
            self.all = self.own + [self.far_up, self.far_down] + self.rest

        def start(self):
            for copy in self.own:
                copy.start()

        def near_up(self):
            self.own[0].wait_recv()
            self.far_up.start()
            self.cross_up.start()

        def near_down(self):
            self.own[1].wait_recv()
            self.far_down.start()
            self.cross_down.start()

        def near_pair(self):
            self.own[2].wait_recv()
            self.other_up.start()
            self.other_down.start()

        def far(self):
            self.far_up.wait_recv()
            self.far_down.wait_recv()
            self.far_pair.start()

        def finish(self):
            for copy in self.rest:
                copy.wait_recv()

        def drain(self):
            for copy in self.all:
                copy.wait_send()

    gathers = [
        [Gather(m, i, columns_of) for i, columns_of in enumerate(column_parts(width, parts))]
        for m, parts in enumerate(GATHER_PARTS)
    ]

    def add_into(m, owner, first, count, sources, cols):
        def step(i, carry):
            at = pl.ds(pl.multiple_of(owner * rows + first + i * CHUNK, CHUNK), CHUNK)
            total = partial[m, at, cols].astype(jnp.float32)
            for source in sources:
                total = total + source[pl.ds(i * CHUNK, CHUNK), cols].astype(jnp.float32)
            partial[m, at, cols] = total.astype(jnp.bfloat16)
            return carry

        lax.fori_loop(0, count // CHUNK, step, 0)

    class Reduce:
        def __init__(self, m, part, columns_of):
            self.m = m
            base = (m * PARTS + part) * PER_PART + REDUCE
            self.whole, self.straight, self.crossing = whole, straight, crossing = columns_of

            def send(owner, number, peer, into, first=0, count=rows, cols=whole):
                return remote(
                    block(partial, m, owner, first, count, cols), into.at[:, cols], base + number, peer
                )

            self.full = full = [got_full.at[m, i] for i in range(6)]
            self.halves = halves = [got_half.at[m, i] for i in range(2)]
            self.crossed = crossed = [got_cross.at[m, i] for i in range(2)]
            self.far_pair = send(c_pair_far, 0, pair, full[0])
            self.other_up = send(c_pair_up, 1, up, full[1], cols=straight)
            self.other_down = send(c_pair_down, 2, down, full[2], cols=straight)
            self.cross_up = send(c_pair_up, 8, pair, crossed[0], cols=crossing)
            self.cross_down = send(c_pair_down, 9, pair, crossed[1], cols=crossing)
            self.hand = remote(block(partial, m, ctx, cols=whole), out_ref.at[m, :, whole], base + 10, after)
            self.far_down = send(c_far, 3, down, halves[0], 0, half)
            self.far_up = send(c_far, 4, up, halves[1], half, half)
            self.near_down = send(c_down, 5, down, full[3])
            self.near_up = send(c_up, 6, up, full[4])
            self.pair = send(c_pair, 7, pair, full[5])
            self.all = [
                self.far_pair,
                self.other_up,
                self.other_down,
                self.far_down,
                self.far_up,
                self.near_down,
                self.near_up,
                self.pair,
                self.cross_up,
                self.cross_down,
            ]

        def start(self):
            self.far_pair.start()
            self.other_up.start()
            self.other_down.start()
            self.cross_up.start()
            self.cross_down.start()

        def add_far(self):
            self.far_pair.wait_recv()
            add_into(self.m, c_far, 0, rows, [self.full[0]], self.whole)
            self.far_down.start()
            self.far_up.start()

        def add_pair(self):
            self.other_up.wait_recv()
            self.other_down.wait_recv()
            add_into(self.m, c_pair, 0, rows, self.full[1:3], self.straight)
            self.pair.start()

        def add_cross(self):
            self.cross_up.wait_recv()
            self.cross_down.wait_recv()
            add_into(self.m, c_up, 0, rows, [self.crossed[0]], self.crossing)
            add_into(self.m, c_down, 0, rows, [self.crossed[1]], self.crossing)

        def add_near(self):
            self.far_down.wait_recv()
            add_into(self.m, c_down, 0, half, [self.halves[0]], self.whole)
            self.near_down.start()
            self.far_up.wait_recv()
            add_into(self.m, c_up, half, half, [self.halves[1]], self.whole)
            self.near_up.start()

        def last(self):
            self.near_down.wait_recv()
            self.near_up.wait_recv()
            self.pair.wait_recv()
            m = self.m
            cols = self.whole
            gate = modulation[pl.ds(m, 1), 2 * width + cols.start : 2 * width + cols.stop]

            def step(i, carry):
                at = pl.ds(pl.multiple_of(ctx * rows + i * CHUNK, CHUNK), CHUNK)
                here = pl.ds(i * CHUNK, CHUNK)
                branch = partial[m, at, cols].astype(jnp.float32)
                for source in self.full[3:]:
                    branch = branch + source[here, cols].astype(jnp.float32)
                result = gathered[m, at, cols].astype(jnp.float32) + gate * branch
                partial[m, at, cols] = result.astype(jnp.bfloat16)
                return carry

            lax.fori_loop(0, rows // CHUNK, step, 0)

            @pl.when(pipe < pipe_count - 1)
            def _():
                self.hand.start()

        def drain(self):
            for copy in self.all:
                copy.wait_send()

    reduces = [
        [Reduce(m, i, columns_of) for i, columns_of in enumerate(column_parts(width, parts))]
        for m, parts in enumerate(REDUCE_PARTS)
    ]

    def finish_modulation():
        layer_load.wait()
        ids = lax.broadcasted_iota(jnp.int32, (8, w_layer.shape[0]), 1)
        chosen = (ids == section_layer[pipe]).astype(jnp.bfloat16)
        layer = jnp.dot(chosen, w_layer[...], preferred_element_type=jnp.float32)
        modulation[...] = mod_total[...] + layer[:clips]

    def rotary_tables():
        cells = jnp.broadcast_to(token_cell[...].astype(jnp.float32), (HEAD, tokens)).T
        columns[...] = cells
        part = 64

        def step(i, carry):
            at = pl.ds(pl.multiple_of(i * part, part), part)
            cell = columns[at].astype(jnp.int32)
            entry = lax.broadcasted_iota(jnp.int32, (part, HEAD), 1)
            pair_id = entry & (HEAD // 2 - 1)
            place = jnp.where(
                pair_id < TIME_PAIRS,
                cell // (GRID_H * GRID_W),
                jnp.where(pair_id < TIME_PAIRS + SPACE_PAIRS, lax.rem(cell // GRID_W, GRID_H), lax.rem(cell, GRID_W)),
            )
            turn = place.astype(jnp.float32) * rates[1:2, :HEAD]
            cos_ref[at] = jnp.cos(turn)
            sin_ref[at] = jnp.where(entry < HEAD // 2, -1.0, 1.0) * jnp.sin(turn)
            return carry

        lax.fori_loop(0, tokens // part, step, 0)

    def norm_block(m, owner):
        shift = modulation[pl.ds(m, 1), 0:width]
        scale = 1.0 + modulation[pl.ds(m, 1), width : 2 * width]

        def step(i, carry):
            at = pl.ds(pl.multiple_of(owner * rows + i * CHUNK, CHUNK), CHUNK)
            values = gathered[m, at].astype(jnp.float32)
            center = values - jnp.mean(values, -1, keepdims=True)
            spread = jnp.mean(center * center, -1, keepdims=True)
            normed[m, at] = (center * lax.rsqrt(spread + 1e-06) * scale + shift).astype(jnp.bfloat16)
            return carry

        lax.fori_loop(0, rows // CHUNK, step, 0, unroll=True)

    def project(m, first, last):
        raw[:, first * local_cols : last * local_cols] = jnp.dot(
            normed[m], w_all[:, first * local_cols : last * local_cols], preferred_element_type=jnp.float32
        )

    stat_sends = [
        [
            remote(stat_own.at[m], stat_got.at[m, s - 1], clips * PARTS * PER_PART + m * STATS + s - 1, ctx_peer(s))
            for s in range(1, CTX)
        ]
        for m in range(clips)
    ]

    def start_stats(m):
        q_raw = raw[:, 0:local_cols]
        k_raw = raw[:, local_cols : 2 * local_cols]
        q_sum = jnp.sum(q_raw * q_raw, -1, keepdims=True)
        k_sum = jnp.sum(k_raw * k_raw, -1, keepdims=True)
        lane = lax.broadcasted_iota(jnp.int32, (tokens, HEAD), 1)
        both = jnp.where(lane == 0, q_sum, k_sum)
        stat_own[m] = both.T[0:2]
        for copy in stat_sends[m]:
            copy.start()

    def finish_stats(m):
        total = stat_own[m]
        for s, copy in enumerate(stat_sends[m]):
            copy.wait_recv()
            total = total + stat_got[m, s]
        inverse = lax.rsqrt(total / width + 1e-06)
        columns[...] = jnp.concatenate([inverse, jnp.zeros((HEAD - 2, tokens), jnp.float32)], 0).T

    def rope(m):
        def step(h, carry):
            for kind, (gain, target) in enumerate(((q_gain, heads_q), (k_gain, heads_k))):
                here = pl.ds(pl.multiple_of(h * HEAD, HEAD), HEAD)
                there = pl.ds(pl.multiple_of(kind * local_cols + h * HEAD, HEAD), HEAD)
                value = raw[:, there] * columns[:, kind : kind + 1] * gain[:, here]
                turned = value * cos_ref[...] + pltpu.roll(value, HEAD // 2, 1) * sin_ref[...]
                target[:, here] = turned.astype(jnp.bfloat16)
            return carry

        lax.fori_loop(0, local_heads, step, 0)
        heads_v[...] = raw[:, 2 * local_cols : 3 * local_cols].astype(jnp.bfloat16)

    q_rows = 256

    def attend(m, head, heads=1):
        def step(i, carry):
            h, r = i // (tokens // q_rows), lax.rem(i, tokens // q_rows)
            here = pl.ds(pl.multiple_of(h * HEAD, HEAD), HEAD)
            at = pl.ds(pl.multiple_of(r * q_rows, q_rows), q_rows)
            scores = lax.dot_general(
                heads_q[at, here], heads_k[:, here], (((1,), (1,)), ((), ())), preferred_element_type=jnp.float32
            ) * HEAD ** (-0.5)
            scores = scores - jnp.max(scores, -1, keepdims=True)
            weights = jnp.exp(scores)
            total = jnp.sum(weights, -1, keepdims=True)
            mixed = jnp.dot(weights.astype(jnp.bfloat16), heads_v[:, here], preferred_element_type=jnp.float32)
            attended[at, here] = (mixed / total).astype(jnp.bfloat16)
            return carry

        lax.fori_loop(head * (tokens // q_rows), (head + heads) * (tokens // q_rows), step, 0)

    out_cols = 512

    def project_out(m, part, parts):
        first, last = (width // out_cols // parts * i for i in (part, part + 1))

        def step(i, carry):
            cols = pl.ds(pl.multiple_of(i * out_cols, out_cols), out_cols)
            partial[m, :, cols] = jnp.dot(
                attended[...], w_out[:, cols], preferred_element_type=jnp.float32
            ).astype(jnp.bfloat16)
            return carry

        lax.fori_loop(first, last, step, 0)

    def mod_slice(ref, index):
        return ref.at[:, pl.ds(pl.multiple_of(index * mod_cols, 128), mod_cols)]

    mod_a = [
        remote(
            mod_slice(mod_part, lax.rem(ctx + s, CTX)), mod_got_a.at[s - 1], s - 1, ctx_peer(s), mod_send, mod_recv
        )
        for s in range(1, CTX)
    ]
    number = CTX - 1
    mod_b = [
        remote(mod_sum.at[0], mod_got_b.at[s - 1], number + s - 1, depth_peer(s), mod_send, mod_recv)
        for s in range(1, depth_pipe)
    ]
    number += depth_pipe - 1
    mod_c = [
        remote(mod_sum.at[1], mod_got_c.at[s - 1], number + s - 1, quad_peer(s), mod_send, mod_recv)
        for s in range(1, lanes_pipe)
    ]
    number += lanes_pipe - 1
    mod_d = [
        remote(mod_slice(mod_total, ctx), mod_slice(mod_total, ctx), number + s - 1, ctx_peer(s), mod_send, mod_recv)
        for s in range(1, CTX)
    ]
    own_cols = pl.ds(pl.multiple_of(ctx * mod_cols, 128), mod_cols)

    def summed(value, copies, got):
        for i, copy in enumerate(copies):
            copy.wait_recv()
            value = value + got[i]
        return value

    for copy in mod_a:
        copy.start()
    g0, g1 = gathers
    r0, r1 = reduces
    for gather in g0:
        gather.start()
    for copy in weights:
        copy.start()
    rotary_tables()
    mod_sum[0] = summed(mod_part[:, own_cols], mod_a, mod_got_a)
    for copy in mod_b:
        copy.start()
    g0[0].near_up()
    g0[0].near_down()
    g0[0].near_pair()
    mod_sum[1] = summed(mod_sum[0], mod_b, mod_got_b)
    for copy in mod_c:
        copy.start()
    g0[1].near_up()
    g0[1].near_down()
    g0[1].near_pair()
    g0[0].far()
    mod_total[:, own_cols] = summed(mod_sum[1], mod_c, mod_got_c)
    for copy in mod_d:
        copy.start()
    g0[1].far()
    for copy in mod_d:
        copy.wait_recv()
    finish_modulation()
    norm_block(1, ctx)
    for gather in g1:
        gather.start()
    for owner in (ctx, c_up, c_down, c_pair, c_far):
        norm_block(0, owner)
    for copy in weights:
        copy.wait()
    for gather in g0:
        gather.finish()
    for owner in (c_pair_up, c_pair_down, c_pair_far):
        norm_block(0, owner)
    project(0, 0, 2)
    g1[0].near_up()
    g1[0].near_down()
    start_stats(0)
    g1[0].near_pair()
    project(0, 2, 3)
    g1[1].near_up()
    g1[1].near_down()
    finish_stats(0)
    g1[1].near_pair()
    rope(0)
    g1[0].far()
    attend(0, 0, 3)
    project_out(0, 0, 2)
    g1[1].far()
    r0[0].start()
    project_out(0, 1, 2)
    r0[1].start()
    for gather in g1:
        gather.finish()
    project(1, 0, 2)
    r0[0].add_pair()
    start_stats(1)
    project(1, 2, 3)
    r0[0].add_far()
    r0[1].add_pair()
    r0[0].add_cross()
    finish_stats(1)
    rope(1)
    r0[0].add_near()
    attend(1, 0)
    r0[1].add_far()
    attend(1, 1)
    r0[1].add_cross()
    attend(1, 2)
    project_out(1, 0, 3)
    r1[0].start()
    project_out(1, 1, 3)
    r1[1].start()
    r0[0].last()
    project_out(1, 2, 3)
    r1[2].start()
    r0[1].add_near()
    r1[0].add_pair()
    r1[0].add_far()
    r1[1].add_pair()
    r1[0].add_cross()
    r1[2].add_pair()
    r1[1].add_far()
    r1[1].add_cross()
    r0[1].last()
    r1[2].add_far()
    r1[2].add_cross()
    for reduce in r1:
        reduce.add_near()
    for reduce in r1:
        reduce.last()

    for gather in g0 + g1:
        gather.drain()
    every = r0 + r1
    for reduce in every:
        reduce.drain()
    for copy in mod_a + mod_b + mod_c + mod_d:
        copy.wait_send()
    for sends in stat_sends:
        for copy in sends:
            copy.wait_send()

    @pl.when(pipe < pipe_count - 1)
    def _():
        for reduce in every:
            reduce.hand.wait_send()

    @pl.when(pipe > 0)
    def _():
        for reduce in every:
            reduce.hand.wait_recv()

    @pl.when(pipe == 0)
    def _():
        out_ref[...] = jnp.zeros_like(out_ref)


def shards(
    inflow,
    patches,
    patch_weight,
    timesteps,
    time_weight,
    mod_weight,
    layer_table,
    section_layer,
    token_cell,
    q_weight,
    k_weight,
    v_weight,
    out_weight,
    q_gain,
    k_gain,
):
    clips, rows, width = inflow.shape[1:]
    local_cols = q_weight.shape[2]
    tokens = rows * CTX
    pipe_count = lax.axis_size("pipe")
    smem = pl.BlockSpec(memory_space=pltpu.SMEM)
    vmem = pl.BlockSpec(memory_space=pltpu.VMEM)
    anywhere = pl.BlockSpec(memory_space=pl.ANY)
    mod_width = mod_weight.shape[1]
    freq_count = time_weight.shape[0]
    time_cols = 32 * mod_weight.shape[0]
    mod_cols = mod_width // CTX
    lanes_pipe = min(4, pipe_count)
    depth_pipe = pipe_count // lanes_pipe
    mod_copies = 2 * (CTX - 1) + depth_pipe - 1 + lanes_pipe - 1
    bf16, f32 = jnp.bfloat16, jnp.float32
    handed = pl.pallas_call(
        functools.partial(section_kernel, pipe_count),
        out_shape=jax.ShapeDtypeStruct((clips, rows, width), bf16),
        in_specs=[smem, smem] + [anywhere] * 4 + [vmem, anywhere, vmem, vmem] + [anywhere] * 4 + [vmem, vmem],
        out_specs=vmem,
        scratch_shapes=[
            pltpu.VMEM((clips, tokens, width), bf16),
            pltpu.VMEM((clips, tokens, width), bf16),
            pltpu.VMEM((width, 3 * local_cols), bf16),
            pltpu.VMEM((local_cols, width), bf16),
            pltpu.VMEM((tokens, 3 * local_cols), f32),
            pltpu.VMEM((tokens, local_cols), bf16),
            pltpu.VMEM((tokens, local_cols), bf16),
            pltpu.VMEM((tokens, local_cols), bf16),
            pltpu.VMEM((tokens, local_cols), bf16),
            pltpu.VMEM((clips, tokens, width), bf16),
            pltpu.VMEM((clips, 6, rows, width), bf16),
            pltpu.VMEM((clips, 2, rows // 2, width), bf16),
            pltpu.VMEM((clips, 2, rows, width), bf16),
            pltpu.VMEM((clips, 2, tokens), f32),
            pltpu.VMEM((clips, CTX - 1, 2, tokens), f32),
            pltpu.VMEM((tokens, HEAD), f32),
            pltpu.VMEM((2, clips, mod_cols), f32),
            pltpu.VMEM((CTX - 1, clips, mod_cols), f32),
            pltpu.VMEM((max(depth_pipe - 1, 1), clips, mod_cols), f32),
            pltpu.VMEM((max(lanes_pipe - 1, 1), clips, mod_cols), f32),
            pltpu.VMEM((clips, mod_width), f32),
            pltpu.VMEM((clips, mod_width), f32),
            pltpu.VMEM((clips, mod_width), f32),
            pltpu.VMEM((tokens, HEAD), f32),
            pltpu.VMEM((tokens, HEAD), f32),
            pltpu.VMEM((freq_count, time_cols), bf16),
            pltpu.VMEM(patch_weight.shape, bf16),
            pltpu.VMEM(layer_table.shape, bf16),
            pltpu.VMEM(patches.shape, bf16),
            pltpu.SemaphoreType.DMA((clips * (PARTS * PER_PART + STATS),)),
            pltpu.SemaphoreType.DMA((clips * (PARTS * PER_PART + STATS),)),
            pltpu.SemaphoreType.DMA((mod_copies,)),
            pltpu.SemaphoreType.DMA((mod_copies,)),
            pltpu.SemaphoreType.DMA((clips + 8,)),
        ],
        compiler_params=pltpu.CompilerParams(
            collective_id=0, has_side_effects=True, vmem_limit_bytes=56 * 2**20
        ),
        cost_estimate=pl.CostEstimate(
            flops=2 * clips * tokens * width * local_cols * 4, bytes_accessed=4 * width * local_cols * 2, transcendentals=0
        ),
    )(
        timesteps,
        section_layer,
        inflow,
        patches,
        patch_weight,
        time_weight,
        mod_weight,
        layer_table,
        token_cell[None],
        rate_rows(freq_count),
        q_weight,
        k_weight,
        v_weight,
        out_weight,
        q_gain,
        k_gain,
    )
    return handed[None]


def solution(mesh):
    placed = (
        P("pipe", None, "ctx", None),
        P(None, "ctx", None),
        P(),
        P(),
        P(),
        P(("pipe", "ctx"), None),
        P(),
        P(),
        P(),
        P("pipe", None, "ctx"),
        P("pipe", None, "ctx"),
        P("pipe", None, "ctx"),
        P("pipe", "ctx", None),
        P("pipe", "ctx"),
        P("pipe", "ctx"),
    )
    return jax.shard_map(
        shards, mesh=mesh, in_specs=placed, out_specs=P("pipe", None, "ctx", None), check_vma=False
    )
```

time: 133 us -> 119 us (0.89); the launches traced: 133 us -> 116 us
  other arithmetic: 7.18 us -> 0 us
  Pallas kernels: 121 us -> 114 us
  matrix products: 2.44 us -> 0 us
    pallas_call x1, Pallas kernels: 121 us -> 114 us  [shards(): pl.pallas_call(functools.partial(section_kernel, pipe_count), out_shape=j...]
    dot_general x3 -> x0, matrix products: 2.44 us -> none  [the longest x1 1.23 us: shards(): jnp.einsum('btp,pd->btd', patches, patch_weight, preferred_element_type=j...]
    reduce_sum x2 -> x0, other arithmetic: 2.3 us -> none  [the longest x1 1.44 us: shards(): layer_id = jnp.sum(jnp.where(section_ids == section, section_layer, 0))]
    neg x1 -> x0, other arithmetic: 1.73 us -> none  [rope_tables(): -sin_half]
where the time goes in v2:
time: 119 us; the launch traced here: 116 us
  Pallas kernels  114 us (96%)
  local copies, waits for them, and re-layouts  2.06 us (2%)
    pallas_call x1, Pallas kernels, shards(): pl.pallas_call(functools.partial(section_kernel, pipe_count), out_shape=j...  114 us

profile of v2, /device:TPU:5, one launch (start us, length us, event | category | flops | bytes accessed | tf_op | source)
XLA Modules:
  0.0 116.5 jit_solution(8800212694053061890)
XLA Ops:
  0.0 114.4 %shard_map.154 = bf16[2,64,3072]{2,1,0:T(8,128)(2,1)} custom-call(s32[2]{0:T(128)} %timesteps.1, s32[32]{0:T(128)} %section_layer.1, bf16[1,2,64,3072]{3,2,1,0:T(8,128)(2,1)} %inflow.1, bf16[2,64,64]{2,1,0:T(8,128)(2,1)} %patches.1, bf16[64,3072]{1,0:T(8,128)(2,1)} %patch_weight.1, bf16[256,3072]{1,0:T(8,128)(2,1)} %time_weight.1, ...), custom_call_target="tpu_custom_call" | custom-call | flops 9663676416 | bytes 9437184 | tf_op jit(solution)/shard_map/pallas_call | solution.py:736
  114.4 2.1 %copy.18 = bf16[1,2,64,3072]{3,2,1,0:T(8,128)(2,1)} copy(bf16[1,2,64,3072]{3,2,1,0:T(8,128)(2,1)} %bitcast.2) | data formatting | bytes 1572864

commit v3 on v2

--- a/solution.py
+++ b/solution.py
@@ -18,8 +18,8 @@
 TIME_PAIRS = HEAD // 2 - 2 * SPACE_PAIRS
 
 GATHER_PARTS = (2, 2)
-REDUCE_PARTS = (2, 3)
-PARTS = 3
+REDUCE_PARTS = (2, 2)
+PARTS = 2
 GATHER = 0
 REDUCE = 10
 PER_PART = 21
@@ -251,6 +251,13 @@
         return ref.at[m, pl.ds(pl.multiple_of(owner * rows + first, 16), count), cols]
 
     half = rows // 2
+    seen = set()
+
+    def arrived(*copies):
+        for copy in copies:
+            if id(copy) not in seen:
+                seen.add(id(copy))
+                copy.wait_recv()
 
     class Gather:
         def __init__(self, m, part, columns_of):
@@ -273,32 +280,34 @@
             self.all = self.own + [self.far_up, self.far_down] + self.rest
 
         def start(self):
-            for copy in self.own:
-                copy.start()
+            self.own[0].start()
+            self.own[1].start()
+
+        def start_pair(self):
+            self.own[2].start()
 
         def near_up(self):
-            self.own[0].wait_recv()
+            arrived(self.own[0])
             self.far_up.start()
             self.cross_up.start()
 
         def near_down(self):
-            self.own[1].wait_recv()
+            arrived(self.own[1])
             self.far_down.start()
             self.cross_down.start()
 
         def near_pair(self):
-            self.own[2].wait_recv()
+            arrived(self.own[2])
             self.other_up.start()
             self.other_down.start()
 
         def far(self):
-            self.far_up.wait_recv()
-            self.far_down.wait_recv()
+            arrived(self.far_up)
+            arrived(self.far_down)
             self.far_pair.start()
 
         def finish(self):
-            for copy in self.rest:
-                copy.wait_recv()
+            arrived(*self.own, self.far_up, self.far_down, *self.rest)
 
         def drain(self):
             for copy in self.all:
@@ -359,42 +368,46 @@
             ]
 
         def start(self):
-            self.far_pair.start()
             self.other_up.start()
             self.other_down.start()
+
+        def start_far(self):
+            self.far_pair.start()
+
+        def start_cross(self):
             self.cross_up.start()
             self.cross_down.start()
 
         def add_far(self):
-            self.far_pair.wait_recv()
+            arrived(self.far_pair)
             add_into(self.m, c_far, 0, rows, [self.full[0]], self.whole)
             self.far_down.start()
             self.far_up.start()
 
         def add_pair(self):
-            self.other_up.wait_recv()
-            self.other_down.wait_recv()
+            arrived(self.other_up)
+            arrived(self.other_down)
             add_into(self.m, c_pair, 0, rows, self.full[1:3], self.straight)
             self.pair.start()
 
         def add_cross(self):
-            self.cross_up.wait_recv()
-            self.cross_down.wait_recv()
+            arrived(self.cross_up)
+            arrived(self.cross_down)
             add_into(self.m, c_up, 0, rows, [self.crossed[0]], self.crossing)
             add_into(self.m, c_down, 0, rows, [self.crossed[1]], self.crossing)
 
         def add_near(self):
-            self.far_down.wait_recv()
+            arrived(self.far_down)
             add_into(self.m, c_down, 0, half, [self.halves[0]], self.whole)
             self.near_down.start()
-            self.far_up.wait_recv()
+            arrived(self.far_up)
             add_into(self.m, c_up, half, half, [self.halves[1]], self.whole)
             self.near_up.start()
 
         def last(self):
-            self.near_down.wait_recv()
-            self.near_up.wait_recv()
-            self.pair.wait_recv()
+            arrived(self.near_down)
+            arrived(self.near_up)
+            arrived(self.pair)
             m = self.m
             cols = self.whole
             gate = modulation[pl.ds(m, 1), 2 * width + cols.start : 2 * width + cols.stop]
@@ -467,10 +480,13 @@
 
         lax.fori_loop(0, rows // CHUNK, step, 0, unroll=True)
 
-    def project(m, first, last):
-        raw[:, first * local_cols : last * local_cols] = jnp.dot(
-            normed[m], w_all[:, first * local_cols : last * local_cols], preferred_element_type=jnp.float32
-        )
+    def project(m):
+        raw[...] = jnp.dot(normed[m], w_all[:, : 2 * local_cols], preferred_element_type=jnp.float32)
+
+    def project_values(m):
+        heads_v[...] = jnp.dot(
+            normed[m], w_all[:, 2 * local_cols :], preferred_element_type=jnp.float32
+        ).astype(jnp.bfloat16)
 
     stat_sends = [
         [
@@ -510,7 +526,6 @@
             return carry
 
         lax.fori_loop(0, local_heads, step, 0)
-        heads_v[...] = raw[:, 2 * local_cols : 3 * local_cols].astype(jnp.bfloat16)
 
     q_rows = 256
 
@@ -556,12 +571,12 @@
     ]
     number = CTX - 1
     mod_b = [
-        remote(mod_sum.at[0], mod_got_b.at[s - 1], number + s - 1, depth_peer(s), mod_send, mod_recv)
+        remote(mod_sum.at[1], mod_got_b.at[s - 1], number + s - 1, depth_peer(s), mod_send, mod_recv)
         for s in range(1, depth_pipe)
     ]
     number += depth_pipe - 1
     mod_c = [
-        remote(mod_sum.at[1], mod_got_c.at[s - 1], number + s - 1, quad_peer(s), mod_send, mod_recv)
+        remote(mod_sum.at[0], mod_got_c.at[s - 1], number + s - 1, quad_peer(s), mod_send, mod_recv)
         for s in range(1, lanes_pipe)
     ]
     number += lanes_pipe - 1
@@ -577,103 +592,121 @@
             value = value + got[i]
         return value
 
+    g0, g1 = gathers
+    r0, r1 = reduces
     for copy in mod_a:
         copy.start()
-    g0, g1 = gathers
-    r0, r1 = reduces
-    for gather in g0:
-        gather.start()
+    g0[1].start()
+    g0[1].start_pair()
+    g0[0].start()
+    mod_sum[0] = summed(mod_part[:, own_cols], mod_a, mod_got_a)
+    for copy in mod_c:
+        copy.start()
+    g0[0].start_pair()
+    g0[1].near_down()
+    mod_sum[1] = summed(mod_sum[0], mod_c, mod_got_c)
+    for copy in mod_b:
+        copy.start()
+    g0[1].near_up()
+    g0[0].near_down()
+    g0[0].near_up()
+    mod_total[:, own_cols] = summed(mod_sum[1], mod_b, mod_got_b)
+    for copy in mod_d:
+        copy.start()
+    g0[1].far()
+    g0[1].near_pair()
+    g0[0].near_pair()
+    g0[0].far()
     for copy in weights:
         copy.start()
     rotary_tables()
-    mod_sum[0] = summed(mod_part[:, own_cols], mod_a, mod_got_a)
-    for copy in mod_b:
-        copy.start()
-    g0[0].near_up()
-    g0[0].near_down()
-    g0[0].near_pair()
-    mod_sum[1] = summed(mod_sum[0], mod_b, mod_got_b)
-    for copy in mod_c:
-        copy.start()
-    g0[1].near_up()
-    g0[1].near_down()
-    g0[1].near_pair()
-    g0[0].far()
-    mod_total[:, own_cols] = summed(mod_sum[1], mod_c, mod_got_c)
-    for copy in mod_d:
-        copy.start()
-    g0[1].far()
     for copy in mod_d:
         copy.wait_recv()
     finish_modulation()
+    arrived(g0[0].own[1], g0[1].own[1])
+    norm_block(0, c_up)
     norm_block(1, ctx)
-    for gather in g1:
-        gather.start()
-    for owner in (ctx, c_up, c_down, c_pair, c_far):
-        norm_block(0, owner)
+    g1[1].start()
+    g1[1].start_pair()
+    arrived(g0[0].own[0], g0[1].own[0])
+    norm_block(0, c_down)
+    arrived(g0[0].own[2], g0[1].own[2])
+    norm_block(0, c_pair)
+    arrived(g0[0].far_up, g0[0].far_down, g0[1].far_up, g0[1].far_down)
+    norm_block(0, c_far)
+    g1[0].start()
+    arrived(g0[0].other_up, g0[0].cross_up, g0[1].other_up, g0[1].cross_up)
+    norm_block(0, c_pair_down)
+    norm_block(0, ctx)
+    arrived(g0[0].other_down, g0[0].cross_down, g0[1].other_down, g0[1].cross_down)
+    norm_block(0, c_pair_up)
+    g1[0].start_pair()
+    arrived(g0[0].far_pair, g0[1].far_pair)
+    norm_block(0, c_pair_far)
     for copy in weights:
         copy.wait()
-    for gather in g0:
-        gather.finish()
-    for owner in (c_pair_up, c_pair_down, c_pair_far):
-        norm_block(0, owner)
-    project(0, 0, 2)
-    g1[0].near_up()
-    g1[0].near_down()
+    project(0)
     start_stats(0)
-    g1[0].near_pair()
-    project(0, 2, 3)
     g1[1].near_up()
     g1[1].near_down()
+    g1[0].near_down()
+    g1[0].near_up()
+    g1[1].near_pair()
+    project_values(0)
+    g1[1].far()
+    g1[0].near_pair()
+    g1[0].far()
     finish_stats(0)
-    g1[1].near_pair()
     rope(0)
-    g1[0].far()
-    attend(0, 0, 3)
+    attend(0, 0)
+    attend(0, 1)
+    attend(0, 2)
     project_out(0, 0, 2)
-    g1[1].far()
+    r0[0].start_far()
     r0[0].start()
     project_out(0, 1, 2)
     r0[1].start()
+    r0[1].start_far()
     for gather in g1:
         gather.finish()
-    project(1, 0, 2)
+    project(1)
+    start_stats(1)
+    r0[0].start_cross()
+    r0[1].start_cross()
+    r0[0].add_far()
     r0[0].add_pair()
-    start_stats(1)
-    project(1, 2, 3)
-    r0[0].add_far()
+    project_values(1)
     r0[1].add_pair()
+    r0[1].add_far()
     r0[0].add_cross()
+    r0[0].add_near()
+    r0[1].add_cross()
     finish_stats(1)
     rope(1)
-    r0[0].add_near()
+    r0[1].add_near()
     attend(1, 0)
-    r0[1].add_far()
     attend(1, 1)
-    r0[1].add_cross()
     attend(1, 2)
-    project_out(1, 0, 3)
+    project_out(1, 0, 2)
+    r1[0].start_far()
     r1[0].start()
-    project_out(1, 1, 3)
+    project_out(1, 1, 2)
+    r0[0].last()
+    r1[1].start_far()
     r1[1].start()
-    r0[0].last()
-    project_out(1, 2, 3)
-    r1[2].start()
-    r0[1].add_near()
+    r0[1].last()
+    r1[0].add_far()
+    r1[0].start_cross()
+    r1[1].start_cross()
+    r1[1].add_far()
+    r1[0].add_cross()
     r1[0].add_pair()
-    r1[0].add_far()
+    r1[0].add_near()
     r1[1].add_pair()
-    r1[0].add_cross()
-    r1[2].add_pair()
-    r1[1].add_far()
     r1[1].add_cross()
-    r0[1].last()
-    r1[2].add_far()
-    r1[2].add_cross()
-    for reduce in r1:
-        reduce.add_near()
-    for reduce in r1:
-        reduce.last()
+    r1[1].add_near()
+    r1[0].last()
+    r1[1].last()
 
     for gather in g0 + g1:
         gather.drain()
@@ -743,7 +776,7 @@
             pltpu.VMEM((clips, tokens, width), bf16),
             pltpu.VMEM((width, 3 * local_cols), bf16),
             pltpu.VMEM((local_cols, width), bf16),
-            pltpu.VMEM((tokens, 3 * local_cols), f32),
+            pltpu.VMEM((tokens, 2 * local_cols), f32),
             pltpu.VMEM((tokens, local_cols), bf16),
             pltpu.VMEM((tokens, local_cols), bf16),
             pltpu.VMEM((tokens, local_cols), bf16),

time: 119 us -> 112 us (0.941)
  Pallas kernels: 114 us -> 108 us
    pallas_call x1, Pallas kernels: 114 us -> 108 us  [shards(): pl.pallas_call(functools.partial(section_kernel, pipe_count), out_shape=j...]
where the time goes in v3:
time: 112 us; the launch traced here: 110 us
  Pallas kernels  108 us (96%)
  local copies, waits for them, and re-layouts  2.06 us (2%)
    pallas_call x1, Pallas kernels, shards(): pl.pallas_call(functools.partial(section_kernel, pipe_count), out_shape=j...  108 us

profile of v3, /device:TPU:5, one launch (start us, length us, event | category | flops | bytes accessed | tf_op | source)
XLA Modules:
  0.0 109.6 jit_solution(11797101917797007910)
XLA Ops:
  0.0 107.6 %shard_map.154 = bf16[2,64,3072]{2,1,0:T(8,128)(2,1)} custom-call(s32[2]{0:T(128)} %timesteps.1, s32[32]{0:T(128)} %section_layer.1, bf16[1,2,64,3072]{3,2,1,0:T(8,128)(2,1)} %inflow.1, bf16[2,64,64]{2,1,0:T(8,128)(2,1)} %patches.1, bf16[64,3072]{1,0:T(8,128)(2,1)} %patch_weight.1, bf16[256,3072]{1,0:T(8,128)(2,1)} %time_weight.1, ...), custom_call_target="tpu_custom_call" | custom-call | flops 9663676416 | bytes 9437184 | tf_op jit(solution)/shard_map/pallas_call | solution.py:769
  107.6 2.1 %copy.18 = bf16[1,2,64,3072]{3,2,1,0:T(8,128)(2,1)} copy(bf16[1,2,64,3072]{3,2,1,0:T(8,128)(2,1)} %bitcast.2) | data formatting | bytes 1572864

commit v4 on v3

--- a/solution.py
+++ b/solution.py
@@ -22,13 +22,14 @@
 PARTS = 2
 GATHER = 0
 REDUCE = 10
-PER_PART = 21
+PER_PART = 22
+CROSSED_REDUCE = False
 STATS = CTX - 1
 
 
-def column_parts(width, parts):
+def column_parts(width, parts, cross_share):
     span = width // parts
-    cross = span // 6 // 128 * 128
+    cross = span // cross_share // 128 * 128
     return [
         (slice(p * span, (p + 1) * span), slice(p * span, (p + 1) * span - cross), slice((p + 1) * span - cross, (p + 1) * span))
         for p in range(parts)
@@ -103,6 +104,7 @@
     w_patch,
     w_layer,
     patch_rows,
+    relay,
     send_sems,
     recv_sems,
     mod_send,
@@ -158,6 +160,11 @@
 
     after = (lax.rem(pipe + 1, pipe_count), ctx)
     before = (lax.rem(pipe + pipe_count - 1, pipe_count), ctx)
+    per_half = pipe_count // 2
+    place = lax.rem(pipe, per_half)
+    half_after = (pipe - place + lax.rem(place + 1, per_half), ctx)
+    half_before = (pipe - place + lax.rem(place + per_half - 1, per_half), ctx)
+    inner, edge, relaying = place < per_half - 1, pipe == per_half - 1, pipe == pipe_count - 1
 
     def own_rows(m):
         return gathered.at[m, pl.ds(pl.multiple_of(ctx * rows, rows), rows)]
@@ -199,7 +206,7 @@
         [ctx_peer(s) for s in range(1, CTX)]
         + [depth_peer(s) for s in range(1, depth_pipe)]
         + [quad_peer(s) for s in range(1, lanes_pipe)]
-        + [after, before]
+        + [after, before, half_after, half_before]
     )
     barrier = pltpu.get_barrier_semaphore()
     for peer in greeted:
@@ -314,7 +321,7 @@
                 copy.wait_send()
 
     gathers = [
-        [Gather(m, i, columns_of) for i, columns_of in enumerate(column_parts(width, parts))]
+        [Gather(m, i, columns_of) for i, columns_of in enumerate(column_parts(width, parts, 6))]
         for m, parts in enumerate(GATHER_PARTS)
     ]
 
@@ -346,9 +353,13 @@
             self.far_pair = send(c_pair_far, 0, pair, full[0])
             self.other_up = send(c_pair_up, 1, up, full[1], cols=straight)
             self.other_down = send(c_pair_down, 2, down, full[2], cols=straight)
-            self.cross_up = send(c_pair_up, 8, pair, crossed[0], cols=crossing)
-            self.cross_down = send(c_pair_down, 9, pair, crossed[1], cols=crossing)
-            self.hand = remote(block(partial, m, ctx, cols=whole), out_ref.at[m, :, whole], base + 10, after)
+            if CROSSED_REDUCE:
+                self.cross_up = send(c_pair_up, 8, pair, crossed[0], cols=crossing)
+                self.cross_down = send(c_pair_down, 9, pair, crossed[1], cols=crossing)
+            result = block(partial, m, ctx, cols=whole)
+            self.hand = remote(result, out_ref.at[m, :, whole], base + 10, after)
+            self.hand_over = remote(result, relay.at[:, whole], base + 11, (pipe_count - 1, ctx))
+            self.hand_on = remote(relay.at[:, whole], out_ref.at[m, :, whole], base + 10, half_after)
             self.far_down = send(c_far, 3, down, halves[0], 0, half)
             self.far_up = send(c_far, 4, up, halves[1], half, half)
             self.near_down = send(c_down, 5, down, full[3])
@@ -363,9 +374,9 @@
                 self.near_down,
                 self.near_up,
                 self.pair,
-                self.cross_up,
-                self.cross_down,
             ]
+            if CROSSED_REDUCE:
+                self.all += [self.cross_up, self.cross_down]
 
         def start(self):
             self.other_up.start()
@@ -375,8 +386,9 @@
             self.far_pair.start()
 
         def start_cross(self):
-            self.cross_up.start()
-            self.cross_down.start()
+            if CROSSED_REDUCE:
+                self.cross_up.start()
+                self.cross_down.start()
 
         def add_far(self):
             arrived(self.far_pair)
@@ -391,6 +403,8 @@
             self.pair.start()
 
         def add_cross(self):
+            if not CROSSED_REDUCE:
+                return
             arrived(self.cross_up)
             arrived(self.cross_down)
             add_into(self.m, c_up, 0, rows, [self.crossed[0]], self.crossing)
@@ -424,16 +438,28 @@
 
             lax.fori_loop(0, rows // CHUNK, step, 0)
 
-            @pl.when(pipe < pipe_count - 1)
+            @pl.when(inner if m == 0 else pipe < pipe_count - 1)
             def _():
                 self.hand.start()
+
+            if m == 0:
+
+                @pl.when(edge)
+                def _():
+                    self.hand_over.start()
+
+        def pass_on(self):
+            @pl.when(relaying)
+            def _():
+                self.hand_over.wait_recv()
+                self.hand_on.start()
 
         def drain(self):
             for copy in self.all:
                 copy.wait_send()
 
     reduces = [
-        [Reduce(m, i, columns_of) for i, columns_of in enumerate(column_parts(width, parts))]
+        [Reduce(m, i, columns_of) for i, columns_of in enumerate(column_parts(width, parts, width))]
         for m, parts in enumerate(REDUCE_PARTS)
     ]
 
@@ -705,33 +731,42 @@
     r1[1].add_pair()
     r1[1].add_cross()
     r1[1].add_near()
+    for copy in mod_a + mod_b + mod_c + mod_d + stat_sends[0] + stat_sends[1]:
+        copy.wait_send()
+    for gather in g0 + g1:
+        gather.drain()
+    for reduce in r0:
+        reduce.drain()
+        reduce.pass_on()
     r1[0].last()
     r1[1].last()
 
-    for gather in g0 + g1:
-        gather.drain()
-    every = r0 + r1
-    for reduce in every:
+    for reduce in r1:
         reduce.drain()
-    for copy in mod_a + mod_b + mod_c + mod_d:
-        copy.wait_send()
-    for sends in stat_sends:
-        for copy in sends:
-            copy.wait_send()
+    @pl.when(inner)
+    def _():
+        for reduce in r0:
+            reduce.hand.wait_send()
+
+    @pl.when(edge)
+    def _():
+        for reduce in r0:
+            reduce.hand_over.wait_send()
+
+    @pl.when(relaying)
+    def _():
+        for reduce in r0:
+            reduce.hand_on.wait_send()
 
     @pl.when(pipe < pipe_count - 1)
     def _():
-        for reduce in every:
+        for reduce in r1:
             reduce.hand.wait_send()
 
     @pl.when(pipe > 0)
     def _():
-        for reduce in every:
+        for reduce in r0 + r1:
             reduce.hand.wait_recv()
-
-    @pl.when(pipe == 0)
-    def _():
-        out_ref[...] = jnp.zeros_like(out_ref)
 
 
 def shards(
@@ -770,7 +805,7 @@
         functools.partial(section_kernel, pipe_count),
         out_shape=jax.ShapeDtypeStruct((clips, rows, width), bf16),
         in_specs=[smem, smem] + [anywhere] * 4 + [vmem, anywhere, vmem, vmem] + [anywhere] * 4 + [vmem, vmem],
-        out_specs=vmem,
+        out_specs=anywhere,
         scratch_shapes=[
             pltpu.VMEM((clips, tokens, width), bf16),
             pltpu.VMEM((clips, tokens, width), bf16),
@@ -801,6 +836,7 @@
             pltpu.VMEM(patch_weight.shape, bf16),
             pltpu.VMEM(layer_table.shape, bf16),
             pltpu.VMEM(patches.shape, bf16),
+            pltpu.VMEM((rows, width), bf16),
             pltpu.SemaphoreType.DMA((clips * (PARTS * PER_PART + STATS),)),
             pltpu.SemaphoreType.DMA((clips * (PARTS * PER_PART + STATS),)),
             pltpu.SemaphoreType.DMA((mod_copies,)),
@@ -831,7 +867,7 @@
         q_gain,
         k_gain,
     )
-    return handed[None]
+    return jnp.where(lax.axis_index("pipe") == 0, 0, handed).astype(bf16)[None]
 
 
 def solution(mesh):

time: 112 us -> 105 us (0.938); the launches traced: 110 us -> 105 us
  Pallas kernels: 108 us -> 103 us
  other arithmetic: 0 us -> 2.08 us
  local copies, waits for them, and re-layouts: 2.06 us -> 0 us
    pallas_call x1, Pallas kernels: 108 us -> 103 us  [shards(): pl.pallas_call(functools.partial(section_kernel, pipe_count), out_shape=j...]
    broadcast_in_dim x0 -> x1, other arithmetic: none -> 2.08 us  [shards(): return jnp.where(lax.axis_index('pipe') == 0, 0, handed).astype(bf16)[None]]
    unnamed x1 -> x0, local copies, waits for them, and re-layouts: 2.06 us -> none
where the time goes in v4:
time: 105 us
  Pallas kernels  103 us (98%)
  other arithmetic  2.08 us (2%)
    pallas_call x1, Pallas kernels, shards(): pl.pallas_call(functools.partial(section_kernel, pipe_count), out_shape=j...  103 us

profile of v4, /device:TPU:5, one launch (start us, length us, event | category | flops | bytes accessed | tf_op | source)
XLA Modules:
  0.0 104.8 jit_solution(5705627094288760761)
XLA Ops:
  0.0 102.8 %shard_map.154 = bf16[2,64,3072]{2,1,0:T(8,128)(2,1)} custom-call(s32[2]{0:T(128)} %timesteps.1, s32[32]{0:T(128)} %section_layer.1, bf16[1,2,64,3072]{3,2,1,0:T(8,128)(2,1)} %inflow.1, bf16[2,64,64]{2,1,0:T(8,128)(2,1)} %patches.1, bf16[64,3072]{1,0:T(8,128)(2,1)} %patch_weight.1, bf16[256,3072]{1,0:T(8,128)(2,1)} %time_weight.1, ...), custom_call_target="tpu_custom_call" | custom-call | flops 9663676416 | bytes 9437184 | tf_op jit(solution)/shard_map/pallas_call | solution.py:804
  102.8 2.1 %select_bitcast_fusion = bf16[1,2,64,3072]{3,2,1,0:T(8,128)(2,1)} fusion(bf16[2,64,3072]{2,1,0:T(8,128)(2,1)} %shard_map.154, pred[]{:T(512)S(6)} %eq.3), kind=kLoop, calls=%fused_computation | loop fusion | flops 393216 | bytes 1572865 | tf_op jit(solution)/shard_map/broadcast_in_dim | solution.py:870

commit v5 on v4

--- a/solution.py
+++ b/solution.py
@@ -321,7 +321,7 @@
                 copy.wait_send()
 
     gathers = [
-        [Gather(m, i, columns_of) for i, columns_of in enumerate(column_parts(width, parts, 6))]
+        [Gather(m, i, columns_of) for i, columns_of in enumerate(column_parts(width, parts, 12))]
         for m, parts in enumerate(GATHER_PARTS)
     ]
 

time: 105 us -> 105 us (level); the launches traced: 105 us -> 103 us
  Pallas kernels: 103 us -> 101 us
    pallas_call x1, Pallas kernels: 103 us -> 101 us  [shards(): pl.pallas_call(functools.partial(section_kernel, pipe_count), out_shape=j...]
where the time goes in v5:
time: 105 us; the launch traced here: 103 us
  Pallas kernels  101 us (96%)
  other arithmetic  2.08 us (2%)
    pallas_call x1, Pallas kernels, shards(): pl.pallas_call(functools.partial(section_kernel, pipe_count), out_shape=j...  101 us

profile of v5, /device:TPU:5, one launch (start us, length us, event | category | flops | bytes accessed | tf_op | source)
XLA Modules:
  0.0 103.3 jit_solution(8061232794019465028)
XLA Ops:
  0.0 101.2 %shard_map.154 = bf16[2,64,3072]{2,1,0:T(8,128)(2,1)} custom-call(s32[2]{0:T(128)} %timesteps.1, s32[32]{0:T(128)} %section_layer.1, bf16[1,2,64,3072]{3,2,1,0:T(8,128)(2,1)} %inflow.1, bf16[2,64,64]{2,1,0:T(8,128)(2,1)} %patches.1, bf16[64,3072]{1,0:T(8,128)(2,1)} %patch_weight.1, bf16[256,3072]{1,0:T(8,128)(2,1)} %time_weight.1, ...), custom_call_target="tpu_custom_call" | custom-call | flops 9663676416 | bytes 9437184 | tf_op jit(solution)/shard_map/pallas_call | solution.py:804
  101.2 2.1 %select_bitcast_fusion = bf16[1,2,64,3072]{3,2,1,0:T(8,128)(2,1)} fusion(bf16[2,64,3072]{2,1,0:T(8,128)(2,1)} %shard_map.154, pred[]{:T(512)S(6)} %eq.3), kind=kLoop, calls=%fused_computation | loop fusion | flops 393216 | bytes 1572865 | tf_op jit(solution)/shard_map/broadcast_in_dim | solution.py:870
